TPU v7x, 128 devices: a whole 4x4x4 slice. The times are simulated.
128 devices in a mesh: drift: 8 (over y, core), cross: 16 (over z, x).
Axes of the slice: x: 4, y: 4, z: 4, core: 2. Of those that a mesh axis runs over, the one named last changes fastest.
Arguments:
- points: float32 [16, 524288], P(None, ('drift', 'cross')), as said below
- send_counts: int32 [16384], P(('drift', 'cross')), may hold values from 1 to 32, as said below
- block_first: int32 [524288], P(('drift', 'cross')), may hold values from 0 to 63
- block_second: int32 [524288], P(('drift', 'cross')), may hold values from 0 to 63
- contact: float32 [524288], P(('drift', 'cross')), may hold values from 0 to 0.9
Outputs:
- final_points: float32 [16, 524288], P(None, ('drift', 'cross'))
- node_velocity: float32 [3, 524288], P(None, ('drift', 'cross'))
Inputs may be any that keep to these rules, and one draw needn't show every extreme that they name: `send_counts`: every device's list of bounds holds the value 32 at least once. `points`: positions lie in 0.52 to 2.48 on every axis and masses are 0.49 or more.
All inputs are finite; a program needn't handle non-finite values.
Results may differ from a plain program's by a relative error of at most 0.0003.
Values sent between devices are 32-bit elements; how exact they have to be, the bound alone decides.
No kernel may reach another device: no remote copies, remote signals or barrier semaphores. Data moves between devices by JAX's collectives and lax.ppermute only.
A program may use at most 128 MiB of HBM per device.

v0:
```python
import jax
import jax.numpy as jnp
from jax import lax
from jax.sharding import PartitionSpec as P

CAP = 32
MIG = 4


step_duration = 0.1
gravity_accel = 1.0


def passed_along(value, axis, steps):
    count = lax.axis_size(axis)
    pairs = [(source, (source + steps) % count) for source in range(count)]
    return lax.ppermute(value, axis, pairs)


def spline(dist):
    size = jnp.abs(dist)
    near = 0.75 - size * size
    far = 0.5 * jnp.square(jnp.maximum(1.5 - size, 0.0))
    return jnp.where(size < 0.5, near, far)


def node_coords():
    index = jnp.arange(64, dtype=jnp.int32)
    return jnp.stack([index // 16, index // 4 % 4, index % 4]).astype(jnp.float32)


def kernel_weights_for(position):
    nodes = jnp.arange(4, dtype=jnp.float32)
    first = spline(position[0][None, :] - nodes[:, None])
    second = spline(position[1][None, :] - nodes[:, None])
    third = spline(position[2][None, :] - nodes[:, None])
    full = first[:, None, None, :] * second[None, :, None, :] * third[None, None, :, :]
    return full.reshape(64, position.shape[1])


def send_out(state, block_ids):
    ids = block_ids.reshape(1, -1)
    got, got_ids = (
        lax.all_to_all(state, ("drift", "cross"), split_axis=1, concat_axis=1, tiled=True),
        lax.all_to_all(ids, ("drift", "cross"), split_axis=1, concat_axis=1, tiled=True),
    )
    return (got, got_ids.reshape(-1))


def send_back(result):
    return lax.all_to_all(result, ("drift", "cross"), split_axis=1, concat_axis=1, tiled=True)


def one_step(state, block_ids, contact):
    resident_blocks = contact.shape[0] // 64
    got, ids = send_out(state, block_ids)
    position = got[0:3]
    velocity = got[3:6]
    affine = got[6:15].reshape(3, 3, -1)
    mass = got[15]
    weight = kernel_weights_for(position)
    offset = node_coords()[:, :, None] - position[:, None, :]
    moved = jnp.einsum("cer,enr->cnr", affine, offset, precision=lax.Precision.HIGHEST)
    momentum = weight[None] * mass[None, None, :] * (velocity[:, None, :] + moved)
    transfer_terms = jnp.concatenate([(weight * mass[None, :])[None], momentum], axis=0)
    block_selector = (ids[:, None] == jnp.arange(resident_blocks, dtype=jnp.int32)[None, :]).astype(
        jnp.float32
    )
    scatter_totals = jnp.einsum(
        "ufv,vg->ugf", transfer_terms, block_selector, precision=lax.Precision.HIGHEST
    ).reshape(4, -1)
    grid_mass = jnp.maximum(scatter_totals[0], 0.5)
    grid_node_velocity = scatter_totals[1:4] / grid_mass[None, :]
    grid_node_velocity = grid_node_velocity.at[2].add(-step_duration * gravity_accel)
    grid_node_velocity = grid_node_velocity * (1.0 - contact)[None, :]
    nodal = jnp.einsum(
        "vlk,gl->vkg",
        grid_node_velocity.reshape(3, resident_blocks, 64),
        block_selector,
        precision=lax.Precision.HIGHEST,
    )
    weighted = weight[None] * nodal
    new_velocity = jnp.sum(weighted, axis=1)
    new_affine = 4.0 * jnp.einsum("cnr,enr->cer", weighted, offset, precision=lax.Precision.HIGHEST)
    new_position = jnp.clip(position + step_duration * new_velocity, 0.5, 2.5)
    result = jnp.concatenate([new_position, new_velocity, new_affine.reshape(9, -1)], axis=0)
    returned = send_back(result)
    kept = jnp.where(state[15:16] > 0.0, returned, state[0:15])
    return (jnp.concatenate([kept, state[15:16]], axis=0), grid_node_velocity)


def local(points, send_counts, block_first, block_second, contact):
    drift_size = lax.axis_size("drift")
    cross_size = lax.axis_size("cross")
    devs = drift_size * cross_size
    slot = jnp.arange(CAP, dtype=jnp.int32)
    live = (slot[None, :] < send_counts[:, None]).astype(jnp.float32).reshape(-1)
    state = points.at[15].multiply(live)
    state, unused = one_step(state, block_first, contact)
    shaped = state.reshape(16, devs, CAP)
    band_cross = passed_along(shaped[:, :, CAP - 2 * MIG : CAP - MIG], "cross", 1)
    band_drift = passed_along(shaped[:, :, CAP - MIG :], "drift", 1)
    shaped = jnp.concatenate([shaped[:, :, : CAP - 2 * MIG], band_cross, band_drift], axis=2)
    state = shaped.reshape(16, -1)
    state, grid_node_velocity = one_step(state, block_second, contact)
    return (state, grid_node_velocity)


def solution(mesh):
    return jax.shard_map(
        local,
        mesh=mesh,
        in_specs=(
            P(None, ("drift", "cross")),
            P(("drift", "cross")),
            P(("drift", "cross")),
            P(("drift", "cross")),
            P(("drift", "cross")),
        ),
        out_specs=(P(None, ("drift", "cross")), P(None, ("drift", "cross"))),
        check_vma=False,
    )
```

profile of v0, /device:TPU:1, one launch (start us, length us, event | category | flops | bytes accessed | tf_op | source)
XLA Modules:
  0.0 355.9 jit_solution(8835956549693187678)
XLA Ops:
  3.0 11.5 %all-to-all-start.1 = ((s32[1,128,32]{2,0,1:T(1,128)}), s32[1,128,32]{2,0,1:T(1,128)S(1)}, u32[]{:S(2)}, u32[]{:S(2)}) async-start(s32[1,128,32]{2,0,1:T(1,128)} %bitcast), calls=%async_computation.1 | async-start | bytes 131072 | tf_op jit(solution)/shard_map/all_to_all | solution.py:45
  18.6 5.7 %all-to-all-done.1 = s32[1,128,32]{2,0,1:T(1,128)S(1)} async-done(((s32[1,128,32]{2,0,1:T(1,128)}), s32[1,128,32]{2,0,1:T(1,128)S(1)}, u32[]{:S(2)}, u32[]{:S(2)}) %all-to-all-start.1) | async-done | bytes 16416 | tf_op jit(solution)/shard_map/all_to_all | solution.py:45
  24.2 4.6 %all-to-all-start = ((f32[128,1,512]{2,1,0:T(1,128)}), f32[128,1,512]{2,1,0:T(1,128)S(1)}, u32[]{:S(2)}, u32[]{:S(2)}) async-start(f32[128,1,512]{2,1,0:T(1,128)} %reshape.760), calls=%async_computation | async-start | bytes 524288 | tf_op jit(solution)/shard_map/all_to_all | solution.py:44
  31.4 8.7 %all-to-all-done = f32[128,1,512]{2,1,0:T(1,128)S(1)} async-done(((f32[128,1,512]{2,1,0:T(1,128)}), f32[128,1,512]{2,1,0:T(1,128)S(1)}, u32[]{:S(2)}, u32[]{:S(2)}) %all-to-all-start) | async-done | bytes 262176 | tf_op jit(solution)/shard_map/all_to_all | solution.py:44
  46.8 5.9 %copy.155 = f32[3,3,4096]{1,0,2:T(4,128)} copy(f32[3,3,4096]{2,1,0:T(4,128)S(1)} %reshape.694) | data formatting | bytes 294912 | tf_op jit(solution)/shard_map/reshape | solution.py:59
  63.0 39.5 %fusion.9 = f32[3,64,4096]{1,0,2:T(4,128)S(1)} fusion(f32[3,3,4096]{1,0,2:T(4,128)} %copy.155, f32[3,4096]{0,1:T(8,128)} %bitcast.74, f32[3,64]{1,0:T(4,128)S(1)} %copy-done.13, f32[3,4096]{0,1:T(8,128)} %bitcast.76, f32[64,4096]{0,1:T(8,128)} %copy.150), kind=kOutput, calls=%fused_computation.13 | convolution fusion | flops 30670848 | bytes 4440832 | tf_op jit(solution)/shard_map/cer,enr->cnr/dot_general | solution.py:63
  102.5 4.6 %pad_maximum_fusion = f32[4,64,4096]{1,0,2:T(4,128)S(1)} fusion(f32[3,64,4096]{1,0,2:T(4,128)S(1)} %fusion.9, f32[1,64,4096]{1,0,2:T(1,128)S(1)} %copy.156), kind=kLoop, calls=%fused_computation.8 | loop fusion | flops 1048576 | bytes 8388608 | tf_op jit(solution)/shard_map/concatenate | solution.py:65
  111.1 3.5 fusion.64
  114.6 6.0 %copy.159 = f32[3,64,4096]{1,0,2:T(4,128)} copy(f32[3,64,4096]{2,1,0:T(8,128)S(1)} %get-tuple-element.55) | data formatting | bytes 6291456 | tf_op jit(solution)/shard_map/mul | solution.py:82
  120.5 31.7 %multiply_bitcast_fusion.1 = f32[3,3,4096]{0,1,2:T(4,128)} fusion(f32[3,64,4096]{1,0,2:T(4,128)} %copy.159, f32[3,4096]{0,1:T(8,128)} %bitcast.75, f32[3,64]{1,0:T(4,128)} %add_convert_fusion), kind=kOutput, calls=%fused_computation.19 | convolution fusion | flops 29134848 | bytes 3343104 | tf_op jit(solution)/shard_map/cnr,enr->cer/dot_general | solution.py:84
  152.3 6.7 %copy.160 = f32[3,3,4096]{2,1,0:T(4,128)S(1)} copy(f32[3,3,4096]{0,1,2:T(4,128)} %multiply_bitcast_fusion.1) | data formatting | bytes 294912 | tf_op jit(solution)/shard_map/mul | solution.py:84
  160.6 15.7 %all_to_all.51 = f32[128,1,480]{2,1,0:T(1,128)S(1)} all-to-all(f32[128,1,480]{2,1,0:T(1,128)S(1)} %reshape.762), channel_id=1, replica_groups=mesh['drift'=8,'cross'=16] {'drift','cross'}, dimensions={0} | all-to-all | bytes 491520 | tf_op jit(solution)/shard_map/all_to_all | solution.py:51
  182.1 7.8 %all-to-all-start.4 = ((s32[1,128,32]{2,0,1:T(1,128)}), s32[1,128,32]{2,0,1:T(1,128)S(1)}, u32[]{:S(2)}, u32[]{:S(2)}) async-start(s32[1,128,32]{2,0,1:T(1,128)} %bitcast.7), calls=%async_computation.4 | async-start | bytes 131072 | tf_op jit(solution)/shard_map/all_to_all | solution.py:45
  194.0 5.6 %all-to-all-done.4 = s32[1,128,32]{2,0,1:T(1,128)S(1)} async-done(((s32[1,128,32]{2,0,1:T(1,128)}), s32[1,128,32]{2,0,1:T(1,128)S(1)}, u32[]{:S(2)}, u32[]{:S(2)}) %all-to-all-start.4) | async-done | bytes 16416 | tf_op jit(solution)/shard_map/all_to_all | solution.py:45
  199.6 4.6 %all-to-all-start.3 = ((f32[128,1,512]{2,1,0:T(1,128)}), f32[128,1,512]{2,1,0:T(1,128)S(1)}, u32[]{:S(2)}, u32[]{:S(2)}) async-start(f32[128,1,512]{2,1,0:T(1,128)} %reshape.764), calls=%async_computation.3 | async-start | bytes 524288 | tf_op jit(solution)/shard_map/all_to_all | solution.py:44
  205.0 10.6 %all-to-all-done.3 = f32[128,1,512]{2,1,0:T(1,128)S(1)} async-done(((f32[128,1,512]{2,1,0:T(1,128)}), f32[128,1,512]{2,1,0:T(1,128)S(1)}, u32[]{:S(2)}, u32[]{:S(2)}) %all-to-all-start.3) | async-done | bytes 262176 | tf_op jit(solution)/shard_map/all_to_all | solution.py:44
  221.6 5.9 %copy.175 = f32[3,3,4096]{1,0,2:T(4,128)} copy(f32[3,3,4096]{2,1,0:T(4,128)S(1)} %reshape.697) | data formatting | bytes 294912 | tf_op jit(solution)/shard_map/reshape | solution.py:59
  237.8 39.5 %fusion.8 = f32[3,64,4096]{1,0,2:T(4,128)S(1)} fusion(f32[3,3,4096]{1,0,2:T(4,128)} %copy.175, f32[3,4096]{0,1:T(8,128)} %bitcast.72, f32[3,4096]{0,1:T(8,128)} %bitcast.77, f32[64,4096]{0,1:T(8,128)} %copy.170, f32[3,64]{1,0:T(4,128)S(1)} %copy-done.14), kind=kOutput, calls=%fused_computation.11 | convolution fusion | flops 30670848 | bytes 4440832 | tf_op jit(solution)/shard_map/cer,enr->cnr/dot_general | solution.py:63
  277.3 4.6 %pad_maximum_fusion.1 = f32[4,64,4096]{1,0,2:T(4,128)S(1)} fusion(f32[3,64,4096]{1,0,2:T(4,128)S(1)} %fusion.8, f32[1,64,4096]{1,0,2:T(1,128)S(1)} %copy.176), kind=kLoop, calls=%fused_computation.9 | loop fusion | flops 1048576 | bytes 8388608 | tf_op jit(solution)/shard_map/concatenate | solution.py:65
  290.0 6.0 %copy.179 = f32[3,64,4096]{1,0,2:T(4,128)} copy(f32[3,64,4096]{2,1,0:T(8,128)S(1)} %get-tuple-element.57) | data formatting | bytes 6291456 | tf_op jit(solution)/shard_map/mul | solution.py:82
  296.0 31.7 %multiply_bitcast_fusion = f32[3,3,4096]{0,1,2:T(4,128)} fusion(f32[3,64,4096]{1,0,2:T(4,128)} %copy.179, f32[3,4096]{0,1:T(8,128)} %bitcast.73, f32[3,64]{1,0:T(4,128)S(1)} %copy-done.14), kind=kOutput, calls=%fused_computation.18 | convolution fusion | flops 29134848 | bytes 3343104 | tf_op jit(solution)/shard_map/cnr,enr->cer/dot_general | solution.py:84
  327.7 6.8 %copy.180 = f32[3,3,4096]{2,1,0:T(4,128)S(1)} copy(f32[3,3,4096]{0,1,2:T(4,128)} %multiply_bitcast_fusion) | data formatting | bytes 294912 | tf_op jit(solution)/shard_map/mul | solution.py:84
  336.8 4.4 %all-to-all-start.5 = ((f32[128,1,480]{2,1,0:T(1,128)}), f32[128,1,480]{2,1,0:T(1,128)S(1)}, u32[]{:S(2)}, u32[]{:S(2)}) async-start(f32[128,1,480]{2,1,0:T(1,128)} %reshape.766), calls=%async_computation.5 | async-start | bytes 524288 | tf_op jit(solution)/shard_map/all_to_all | solution.py:51
  341.9 10.7 %all-to-all-done.5 = f32[128,1,480]{2,1,0:T(1,128)S(1)} async-done(((f32[128,1,480]{2,1,0:T(1,128)}), f32[128,1,480]{2,1,0:T(1,128)S(1)}, u32[]{:S(2)}, u32[]{:S(2)}) %all-to-all-start.5) | async-done | bytes 245792 | tf_op jit(solution)/shard_map/all_to_all | solution.py:51
  (163 shorter events, 72.2 us)
Async XLA Ops:
  3.0 21.2 %all-to-all-start.1 = ((s32[1,128,32]{2,0,1:T(1,128)}), s32[1,128,32]{2,0,1:T(1,128)S(1)}, u32[]{:S(2)}, u32[]{:S(2)}) async-start(s32[1,128,32]{2,0,1:T(1,128)} %bitcast), calls=%async_computation.1 | async-start | bytes 131072 | tf_op jit(solution)/shard_map/all_to_all | solution.py:45
  24.2 15.9 %all-to-all-start = ((f32[128,1,512]{2,1,0:T(1,128)}), f32[128,1,512]{2,1,0:T(1,128)S(1)}, u32[]{:S(2)}, u32[]{:S(2)}) async-start(f32[128,1,512]{2,1,0:T(1,128)} %reshape.760), calls=%async_computation | async-start | bytes 524288 | tf_op jit(solution)/shard_map/all_to_all | solution.py:44
  44.9 12.3 %copy-start.3 = (f32[64,4096]{1,0:T(8,128)}, f32[64,4096]{1,0:T(8,128)S(1)}, u32[]{:S(2)}) copy-start(f32[64,4096]{1,0:T(8,128)S(1)} %mul.326) | copy-start | bytes 3145732
  46.3 6.5 %copy-start.4 = (f32[3,128,32]{2,0,1:T(4,128)S(1)}, f32[3,128,32]{2,0,1:T(4,128)}, u32[]{:S(2)}) copy-start(f32[3,128,32]{2,0,1:T(4,128)} %get-tuple-element.53) | copy-start | bytes 147460
  46.4 8.5 %copy-start.6 = (f32[3,128,32]{2,0,1:T(4,128)S(1)}, f32[3,128,32]{2,0,1:T(4,128)}, u32[]{:S(2)}) copy-start(f32[3,128,32]{2,0,1:T(4,128)} %get-tuple-element.52) | copy-start | bytes 147460
  52.7 10.3 %copy-start.13 = (f32[3,64]{1,0:T(4,128)S(1)}, f32[3,64]{1,0:T(4,128)}, u32[]{:S(2)}) copy-start(f32[3,64]{1,0:T(4,128)} %add_convert_fusion) | copy-start | bytes 2308
  152.2 7.0 %copy-start.9 = (f32[3,4096]{1,0:T(4,128)S(1)}, f32[3,4096]{1,0:T(4,128)}, u32[]{:S(2)}) copy-start(f32[3,4096]{1,0:T(4,128)} %get-tuple-element.54) | copy-start | bytes 147460
  152.3 7.1 %copy-start.5 = (f32[3,128,32]{2,0,1:T(4,128)S(1)}, f32[3,128,32]{2,0,1:T(4,128)}, u32[]{:S(2)}) copy-start(f32[3,128,32]{2,0,1:T(4,128)} %get-tuple-element.53) | copy-start | bytes 147460
  159.0 19.6 %copy-start.11 = (pred[4096]{0:T(1024)(128)(4,1)S(1)}, pred[4096]{0:T(1024)(128)(4,1)}, u32[]{:S(2)}) copy-start(pred[4096]{0:T(1024)(128)(4,1)} %get-tuple-element.46) | copy-start | bytes 12292
  160.1 21.3 %copy-start.12 = (s32[4096]{0:T(1024)S(1)}, s32[4096]{0:T(1024)}, u32[]{:S(2)}) copy-start(s32[4096]{0:T(1024)} %param.14) | copy-start | bytes 49156
  180.0 9.9 %collective-permute-start.1 = (f32[16,128,4]{1,0,2:T(8,128)S(1)}, f32[16,128,4]{1,0,2:T(8,128)S(1)}, u32[]{:S(2)}, u32[]{:S(2)}) collective-permute-start(f32[16,128,4]{1,0,2:T(8,128)S(1)} %copy.164), channel_id=1, source_target_pairs={{0,16},{16,32},{32,48},{48,64},{64,80},{80,96},{96,112},{112,0},{1... | collective-permute-start | bytes 98312 | tf_op jit(solution)/shard_map/ppermute | solution.py:17
  181.0 9.2 %collective-permute-start = (f32[16,128,4]{1,0,2:T(8,128)S(1)}, f32[16,128,4]{1,0,2:T(8,128)S(1)}, u32[]{:S(2)}, u32[]{:S(2)}) collective-permute-start(f32[16,128,4]{1,0,2:T(8,128)S(1)} %copy.163), channel_id=1, source_target_pairs={{0,1},{1,2},{2,3},{3,4},{4,5},{5,6},{6,7},{7,8},{8,9},{9,10},{10,1... | collective-permute-start | bytes 98312 | tf_op jit(solution)/shard_map/ppermute | solution.py:17
  182.1 17.5 %all-to-all-start.4 = ((s32[1,128,32]{2,0,1:T(1,128)}), s32[1,128,32]{2,0,1:T(1,128)S(1)}, u32[]{:S(2)}, u32[]{:S(2)}) async-start(s32[1,128,32]{2,0,1:T(1,128)} %bitcast.7), calls=%async_computation.4 | async-start | bytes 131072 | tf_op jit(solution)/shard_map/all_to_all | solution.py:45
  191.2 1.0 copy-start
  199.6 15.9 %all-to-all-start.3 = ((f32[128,1,512]{2,1,0:T(1,128)}), f32[128,1,512]{2,1,0:T(1,128)S(1)}, u32[]{:S(2)}, u32[]{:S(2)}) async-start(f32[128,1,512]{2,1,0:T(1,128)} %reshape.764), calls=%async_computation.3 | async-start | bytes 524288 | tf_op jit(solution)/shard_map/all_to_all | solution.py:44
  219.7 12.3 %copy-start.2 = (f32[64,4096]{1,0:T(8,128)}, f32[64,4096]{1,0:T(8,128)S(1)}, u32[]{:S(2)}) copy-start(f32[64,4096]{1,0:T(8,128)S(1)} %mul.354) | copy-start | bytes 3145732
  221.1 8.6 %copy-start.7 = (f32[3,128,32]{2,0,1:T(4,128)S(1)}, f32[3,128,32]{2,0,1:T(4,128)}, u32[]{:S(2)}) copy-start(f32[3,128,32]{2,0,1:T(4,128)} %get-tuple-element.48) | copy-start | bytes 147460
  227.5 10.3 %copy-start.14 = (f32[3,64]{1,0:T(4,128)S(1)}, f32[3,64]{1,0:T(4,128)}, u32[]{:S(2)}) copy-start(f32[3,64]{1,0:T(4,128)} %add_convert_fusion) | copy-start | bytes 2308
  285.8 0.6 copy-start.10
  327.6 7.1 %copy-start.8 = (f32[3,4096]{1,0:T(4,128)S(1)}, f32[3,4096]{1,0:T(4,128)}, u32[]{:S(2)}) copy-start(f32[3,4096]{1,0:T(4,128)} %get-tuple-element.56) | copy-start | bytes 147460
  327.7 13.5 %slice-start = ((f32[16,128,32]{2,1,0:T(8,128)}), f32[1,128,32]{2,1,0:T(8,128)S(1)}, s32[]{:S(2)}) async-start(f32[16,128,32]{2,1,0:T(8,128)} %copy-done), calls=%async_computation.6 | async-start | bytes 131072 | tf_op jit(solution)/shard_map/slice | solution.py:88
  327.7 13.7 %slice-start.1 = ((f32[16,128,32]{2,1,0:T(8,128)}), f32[15,128,32]{2,1,0:T(8,128)S(1)}, s32[]{:S(2)}) async-start(f32[16,128,32]{2,1,0:T(8,128)} %copy-done), calls=%async_computation.7 | async-start | bytes 1966080 | tf_op jit(solution)/shard_map/slice | solution.py:88
  327.7 14.1 %copy-start.1 = (f32[16,128,32]{2,1,0:T(8,128)S(1)}, f32[16,128,32]{2,1,0:T(8,128)}, u32[]{:S(2)}) copy-start(f32[16,128,32]{2,1,0:T(8,128)} %copy-done) | copy-start | bytes 786436
  336.8 15.8 %all-to-all-start.5 = ((f32[128,1,480]{2,1,0:T(1,128)}), f32[128,1,480]{2,1,0:T(1,128)S(1)}, u32[]{:S(2)}, u32[]{:S(2)}) async-start(f32[128,1,480]{2,1,0:T(1,128)} %reshape.766), calls=%async_computation.5 | async-start | bytes 524288 | tf_op jit(solution)/shard_map/all_to_all | solution.py:51
where the time goes:
time: 360 us; the launch traced here: 356 us
  matrix products  156 us (43%)
  local copies, waits for them, and re-layouts  83.9 us (23%)
  waiting for transfers between devices  41.2 us (11%)
  starting transfers between devices  33.9 us (9%)
  other arithmetic  23.6 us (7%)
  blocking collectives  15.7 us (4%)
    dot_general x2, matrix products, one_step(): jnp.einsum('cer,enr->cnr', affine, offset, precision=lax.Precision.HIGHEST)  78.9 us
    dot_general x2, matrix products, one_step(): jnp.einsum('cnr,enr->cer', weighted, offset, precision=lax.Precision.HIGH...  63.4 us
    all_to_all x2, waiting for transfers between devices, send_out(): lax.all_to_all(state, ('drift', 'cross'), split_axis=1, concat_axis=1, ti...  19.3 us
    all_to_all x2, starting transfers between devices, send_out(): lax.all_to_all(ids, ('drift', 'cross'), split_axis=1, concat_axis=1, tile...  19.3 us
    all_to_all x1, blocking collectives, send_back(): lax.all_to_all(result, ('drift', 'cross'), split_axis=1, concat_axis=1, t...  15.7 us
    mul x2, local copies, waits for them, and re-layouts, one_step(): 4.0 * jnp.einsum('cnr,enr->cer', weighted, offset, precision=lax.Precisio...  13.6 us
    reshape x4, local copies, waits for them, and re-layouts, one_step(): affine = got[6:15].reshape(3, 3, -1)  12.5 us
    mul x2, local copies, waits for them, and re-layouts, one_step(): weighted = weight[None] * nodal  11.9 us
  transfers between devices with their start and end apart: 7, of which 5 were waited for; matrix products, arithmetic and copies ran while one was open for 3% of the time, Pallas kernels for 0%

commit v1 on v0

v1 whole, which is shorter than its diff:
```python
import jax
import jax.numpy as jnp
from jax import lax
from jax.experimental import pallas as pl
from jax.experimental.pallas import tpu as pltpu
from jax.sharding import PartitionSpec as P

CAP = 32
MIG = 4
NODES = 64
BLK_DEV = 64
DEVS = 128
N_CROSS = 16
LANES = 128

STEP_DURATION = 0.1
GRAVITY_ACCEL = 1.0

SEND_ROWS = 5
BACK_ROWS = 4

VMEM_LIMIT = 32 * 1024 * 1024


def spline(dist):
    size = jnp.abs(dist)
    near = 0.75 - size * size
    far = 0.5 * jnp.square(jnp.maximum(1.5 - size, 0.0))
    return jnp.where(size < 0.5, near, far)


def pack_kernel(points_ref, counts_ref, first_ref, second_ref, out_ref, counts_col):
    counts = counts_ref[...].astype(jnp.float32)
    counts_col[...] = jnp.broadcast_to(counts, (DEVS, LANES)).T
    lane = lax.broadcasted_iota(jnp.int32, (32, LANES), 1)
    part = lane // CAP

    def feature(f):
        if f < 16:
            return points_ref[f // 8, :, f % 8, :]
        return (first_ref if f == 16 else second_ref)[...].astype(jnp.float32)

    for j in range(SEND_ROWS):
        rows = [feature(4 * j + ff) for ff in range(4) if 4 * j + ff < 18]
        for oo in range(4):
            block = jnp.zeros((32, LANES), jnp.float32)
            for ff, row in enumerate(rows):
                moved = pltpu.roll(row, ((ff - oo) * CAP) % LANES, 1) if ff != oo else row
                block = jnp.where(part == ff, moved, block)
            if j == 3:
                count = counts_col[pl.ds(oo, 32, stride=4), :]
                slot = (lane - 3 * CAP).astype(jnp.float32)
                live = (slot < count).astype(jnp.float32)
                block = jnp.where(part == 3, block * live, block)
            out_ref[pl.ds(SEND_ROWS * oo + j, 32, stride=4 * SEND_ROWS), :] = block


def unpack_kernel(back_ref, out_ref):
    lane = lax.broadcasted_iota(jnp.int32, (32, LANES), 1)
    part = lane // CAP
    for j in range(BACK_ROWS):
        blocks = [back_ref[pl.ds(BACK_ROWS * oo + j, 32, stride=4 * BACK_ROWS), :] for oo in range(4)]
        for ff in range(4):
            f = 4 * j + ff
            row = blocks[0]
            for oo, block in enumerate(blocks):
                moved = pltpu.roll(block, ((oo - ff) * CAP) % LANES, 1) if ff != oo else block
                row = jnp.where(part == oo, moved, row)
            out_ref[f // 8, :, f % 8, :] = row


def steps_kernel(
    got_ref, contact_ref, back_ref, vel_ref, state, terms, patterns, sums, selector, parts, reduced, keep, pairs
):
    def rows_of(f):
        return state[f * CAP : (f + 1) * CAP, :]

    def put(f, value):
        state[f * CAP : (f + 1) * CAP, :] = value

    for j in range(SEND_ROWS):
        state[j * LANES : (j + 1) * LANES, :] = got_ref[pl.ds(j, DEVS, stride=SEND_ROWS), :].T

    contact = contact_ref[...]
    pairs[pl.ds(0, 32, stride=2), :] = contact
    pairs[pl.ds(1, 32, stride=2), :] = pltpu.roll(contact, NODES, 1)
    turned = jnp.concatenate([pairs[...], pairs[...]], axis=0).T
    keep[...] = 1.0 - turned[0:NODES, :]

    sub = lax.broadcasted_iota(jnp.int32, (8, LANES), 0)
    k_of = (sub % 4).astype(jnp.float32)
    j_of = (sub // 4).astype(jnp.float32)
    block_of = lax.broadcasted_iota(jnp.int32, (BLK_DEV, LANES), 0).astype(jnp.float32)
    half = lax.broadcasted_iota(jnp.int32, (3 * NODES, LANES), 1) < BLK_DEV

    def one_step(ids_row):
        position = [rows_of(e) for e in range(3)]
        velocity = [rows_of(3 + c) for c in range(3)]
        affine = [[rows_of(6 + 3 * c + e) for e in range(3)] for c in range(3)]
        mass = rows_of(15)

        def put_term(q, value):
            terms[q * CAP : (q + 1) * CAP, :] = value

        put_term(0, mass)
        for c in range(3):
            moved = affine[c][0] * position[0] + affine[c][1] * position[1] + affine[c][2] * position[2]
            put_term(1 + c, velocity[c] - moved)
            for e in range(3):
                put_term(4 + 3 * c + e, affine[c][e])
        for i in range(4):
            put_term(13 + i, spline(position[0] - float(i)))
        middle = [spline(position[1] - float(i)) for i in range(4)]
        last = [spline(position[2] - float(i)) for i in range(4)]
        for r in range(8):
            patterns[r * CAP : (r + 1) * CAP, :] = last[r % 4]
            patterns[(8 + r) * CAP : (9 + r) * CAP, :] = middle[r // 4]
            patterns[(16 + r) * CAP : (17 + r) * CAP, :] = middle[2 + r // 4]

        def term(q, c):
            return terms[pl.ds(q * CAP + c, 1), :]

        def pair_weights(c):
            third = patterns[pl.ds(c, 8, stride=CAP), :]
            return [patterns[pl.ds(8 * (1 + h) * CAP + c, 8, stride=CAP), :] * third for h in range(2)]

        sums[...] = jnp.zeros_like(sums)

        def scatter(c, unused):
            ids = state[pl.ds(ids_row * CAP + c, 1), :]
            chosen = jnp.where(block_of == ids, 1.0, 0.0).astype(jnp.bfloat16)
            selector[c] = chosen
            inner = [w * term(0, c) for w in pair_weights(c)]
            weights = [term(13 + i, c) * inner[h] for i in range(4) for h in range(2)]
            pieces = list(weights)
            for v in range(3):
                along = term(4 + 3 * v, c)
                start = term(1 + v, c) + term(6 + 3 * v, c) * k_of
                middle_term = term(5 + 3 * v, c)
                at = [start + middle_term * j_of, start + middle_term * (j_of + 2.0)]
                for i in range(4):
                    for h in range(2):
                        pieces.append(weights[2 * i + h] * at[h])
                    at = [a + along for a in at]
            full = jnp.concatenate(pieces, axis=0)
            high = full.astype(jnp.bfloat16)
            low = (full - high.astype(jnp.float32)).astype(jnp.bfloat16)
            twice = jnp.concatenate([chosen, chosen], axis=0)
            sums[...] += lax.dot_general(
                jnp.concatenate([high, low], axis=1),
                jnp.concatenate([twice, twice], axis=1),
                (((1,), (1,)), ((), ())),
                preferred_element_type=jnp.float32,
            )
            return unused

        lax.fori_loop(0, CAP, scatter, 0)

        grid_mass = jnp.maximum(sums[0:NODES, :], 0.5)
        node = []
        for v in range(3):
            value = sums[(1 + v) * NODES : (2 + v) * NODES, :] / grid_mass
            if v == 2:
                value = value - STEP_DURATION * GRAVITY_ACCEL
            node.append(value * keep[...])
        whole = jnp.concatenate(node, axis=0)
        first = whole.astype(jnp.bfloat16).astype(jnp.float32)
        rest = whole - first
        second = rest.astype(jnp.bfloat16).astype(jnp.float32)
        third = jnp.where(half, rest - second, 0.0)
        parts[:, 0:LANES] = jnp.where(half, first, second).astype(jnp.bfloat16)
        parts[:, LANES : 2 * LANES] = third.astype(jnp.bfloat16)

        def gather(c, unused):
            chosen = selector[c]
            nodal = jnp.dot(
                parts[...],
                jnp.concatenate([chosen, chosen, chosen, chosen], axis=0),
                preferred_element_type=jnp.float32,
            )
            inner = pair_weights(c)
            weights = [term(13 + i, c) * inner[h] for i in range(4) for h in range(2)]
            for v in range(3):
                weighted = [
                    weights[n] * nodal[v * NODES + 8 * n : v * NODES + 8 * (n + 1), :] for n in range(8)
                ]
                by_i = [weighted[2 * i] + weighted[2 * i + 1] for i in range(4)]
                odd = (weighted[1] + weighted[3]) + (weighted[5] + weighted[7])
                outer = by_i[2] + by_i[3]
                total = (by_i[0] + by_i[1]) + outer
                first_moment = (by_i[1] + by_i[3]) + (outer + outer)
                for t, value in enumerate((total, odd, first_moment)):
                    reduced[pl.ds((3 * v + t) * 8 * CAP + c * 8, 8), :] = value
            return unused

        lax.fori_loop(0, CAP, gather, 0)

        def spread(v, t):
            return [reduced[pl.ds((3 * v + t) * 8 * CAP + r, CAP, stride=8), :] for r in range(8)]

        def add_all(values):
            total = values[0]
            for value in values[1:]:
                total = total + value
            return total

        alive = mass > 0.0
        for v in range(3):
            by_row = spread(v, 0)
            by_k = [by_row[k] + by_row[4 + k] for k in range(4)]
            new_velocity = (by_k[0] + by_k[1]) + (by_k[2] + by_k[3])
            moment = [
                add_all(spread(v, 2)),
                2.0 * add_all(spread(v, 1)) + add_all(by_row[4:]),
                (by_k[1] + by_k[3]) + 2.0 * (by_k[2] + by_k[3]),
            ]
            for e in range(3):
                new_affine = 4.0 * (moment[e] - position[e] * new_velocity)
                put(6 + 3 * v + e, jnp.where(alive, new_affine, affine[v][e]))
            put(3 + v, jnp.where(alive, new_velocity, velocity[v]))
            new_position = jnp.clip(position[v] + STEP_DURATION * new_velocity, 0.5, 2.5)
            put(v, jnp.where(alive, new_position, position[v]))
        return node

    one_step(16)

    source = lax.broadcasted_iota(jnp.int32, (2 * MIG, LANES), 1)
    slot = lax.broadcasted_iota(jnp.int32, (2 * MIG, LANES), 0)
    for f in range(16):
        at = f * CAP + CAP - 2 * MIG
        old = state[at : at + 2 * MIG, :]
        across = jnp.where(
            source % N_CROSS == 0, pltpu.roll(old, LANES - (N_CROSS - 1), 1), pltpu.roll(old, 1, 1)
        )
        state[at : at + 2 * MIG, :] = jnp.where(slot < MIG, across, pltpu.roll(old, N_CROSS, 1))

    node = one_step(17)

    for j in range(BACK_ROWS):
        back_ref[pl.ds(j, DEVS, stride=BACK_ROWS), :] = state[j * LANES : (j + 1) * LANES, :].T

    lane = lax.broadcasted_iota(jnp.int32, (32, LANES), 1)
    for v in range(3):
        pairs[...] = jnp.concatenate([node[v], node[v]], axis=0).T[0:BLK_DEV, :]
        packed = jnp.where(lane < NODES, pairs[pl.ds(0, 32, stride=2), :], pairs[pl.ds(1, 32, stride=2), :])
        for q in range(32):
            vel_ref[v : v + 1, q * LANES : (q + 1) * LANES] = packed[q : q + 1, :]


def in_vmem(count):
    return [pl.BlockSpec(memory_space=pltpu.VMEM)] * count


def local(points, send_counts, block_first, block_second, contact):
    params = pltpu.CompilerParams(vmem_limit_bytes=VMEM_LIMIT)
    tiled = points.reshape(2, 8, 32, LANES).transpose(0, 2, 1, 3)
    send = pl.pallas_call(
        pack_kernel,
        out_shape=jax.ShapeDtypeStruct((DEVS * SEND_ROWS, LANES), jnp.float32),
        in_specs=in_vmem(4),
        out_specs=in_vmem(1)[0],
        scratch_shapes=[pltpu.VMEM((DEVS, LANES), jnp.float32)],
        compiler_params=params,
    )(tiled, send_counts.reshape(1, DEVS), block_first.reshape(32, LANES), block_second.reshape(32, LANES))
    got = lax.all_to_all(
        send.reshape(DEVS, 1, SEND_ROWS * LANES), ("drift", "cross"), split_axis=0, concat_axis=0, tiled=True
    )
    back, node_velocity = pl.pallas_call(
        steps_kernel,
        out_shape=(
            jax.ShapeDtypeStruct((DEVS * BACK_ROWS, LANES), jnp.float32),
            jax.ShapeDtypeStruct((3, BLK_DEV * NODES), jnp.float32),
        ),
        in_specs=in_vmem(2),
        out_specs=tuple(in_vmem(2)),
        scratch_shapes=[
            pltpu.VMEM((SEND_ROWS * LANES, LANES), jnp.float32),
            pltpu.VMEM((17 * CAP, LANES), jnp.float32),
            pltpu.VMEM((24 * CAP, LANES), jnp.float32),
            pltpu.VMEM((4 * NODES, LANES), jnp.float32),
            pltpu.VMEM((CAP, BLK_DEV, LANES), jnp.bfloat16),
            pltpu.VMEM((3 * NODES, 2 * LANES), jnp.bfloat16),
            pltpu.VMEM((9 * 8 * CAP, LANES), jnp.float32),
            pltpu.VMEM((NODES, LANES), jnp.float32),
            pltpu.VMEM((BLK_DEV, LANES), jnp.float32),
        ],
        compiler_params=params,
    )(got.reshape(DEVS * SEND_ROWS, LANES), contact.reshape(32, LANES))
    returned = lax.all_to_all(
        back.reshape(DEVS, 1, BACK_ROWS * LANES), ("drift", "cross"), split_axis=0, concat_axis=0, tiled=True
    )
    final = pl.pallas_call(
        unpack_kernel,
        out_shape=jax.ShapeDtypeStruct((2, 32, 8, LANES), jnp.float32),
        in_specs=in_vmem(1),
        out_specs=in_vmem(1)[0],
        compiler_params=params,
    )(returned.reshape(DEVS * BACK_ROWS, LANES))
    return (final.transpose(0, 2, 1, 3).reshape(16, DEVS * CAP), node_velocity)


def solution(mesh):
    return jax.shard_map(
        local,
        mesh=mesh,
        in_specs=(
            P(None, ("drift", "cross")),
            P(("drift", "cross")),
            P(("drift", "cross")),
            P(("drift", "cross")),
            P(("drift", "cross")),
        ),
        out_specs=(P(None, ("drift", "cross")), P(None, ("drift", "cross"))),
        check_vma=False,
    )
```

time: 360 us -> 69 us (0.19); the launches traced: 356 us -> 68.7 us
  matrix products: 156 us -> 0 us
  local copies, waits for them, and re-layouts: 83.9 us -> 3.04 us
  waiting for transfers between devices: 41.2 us -> 0 us
  starting transfers between devices: 33.9 us -> 0 us
  Pallas kernels: 0 us -> 26.3 us
  other arithmetic: 23.6 us -> 0 us
  blocking collectives: 15.7 us -> 38.7 us
    dot_general x8 -> x0, matrix products: 156 us -> none  [the longest x2 78.9 us: one_step(): jnp.einsum('cer,enr->cnr', affine, offset, precision=lax.Precision.HIGHEST)]
    all_to_all x5 -> x0, waiting for transfers between devices: 41.2 us -> none  [the longest x2 19.3 us: send_out(): lax.all_to_all(state, ('drift', 'cross'), split_axis=1, concat_axis=1, ti...]
    mul x14 -> x0, local copies, waits for them, and re-layouts: 37.9 us -> none  [the longest x2 13.6 us: one_step(): 4.0 * jnp.einsum('cnr,enr->cer', weighted, offset, precision=lax.Precisio...]
    all_to_all x5 -> x0, starting transfers between devices: 32.8 us -> none  [the longest x2 19.3 us: send_out(): lax.all_to_all(ids, ('drift', 'cross'), split_axis=1, concat_axis=1, tile...]
    pallas_call x0 -> x3, Pallas kernels: none -> 26.3 us  [the longest x1 24.9 us: local(): pl.pallas_call(steps_kernel, out_shape=(jax.ShapeDtypeStruct((DEVS * BACK...]
    all_to_all x1 -> x2, blocking collectives: 15.7 us -> 38.7 us  [the longest x1 23.4 us: local(): lax.all_to_all(send.reshape(DEVS, 1, SEND_ROWS * LANES), ('drift', 'cross...]
    reshape x7 -> x0, local copies, waits for them, and re-layouts: 13.1 us -> none  [the longest x4 12.5 us: one_step(): affine = got[6:15].reshape(3, 3, -1)]
    concatenate x7 -> x0, other arithmetic: 10.8 us -> none  [the longest x2 9.23 us: one_step(): jnp.concatenate([(weight * mass[None, :])[None], momentum], axis=0)]
  transfers between devices with their start and end apart: 7 -> 0, of which waited for: 5 -> 0; matrix products, arithmetic and copies ran while one was open for 3% -> 0% of each run, Pallas kernels for 0% -> 0%
where the time goes in v1:
time: 69 us; the launch traced here: 68.7 us
  blocking collectives  38.7 us (56%)
  Pallas kernels  26.3 us (38%)
  local copies, waits for them, and re-layouts  3.04 us (4%)
    pallas_call x1, Pallas kernels, local(): pl.pallas_call(steps_kernel, out_shape=(jax.ShapeDtypeStruct((DEVS * BACK...  24.9 us
    all_to_all x1, blocking collectives, local(): lax.all_to_all(send.reshape(DEVS, 1, SEND_ROWS * LANES), ('drift', 'cross...  23.4 us
    all_to_all x1, blocking collectives, local(): lax.all_to_all(back.reshape(DEVS, 1, BACK_ROWS * LANES), ('drift', 'cross...  15.3 us
    unnamed x10, local copies, waits for them, and re-layouts  3.04 us

profile of v1, /device:TPU:1, one launch (start us, length us, event | category | flops | bytes accessed | tf_op | source)
XLA Modules:
  0.0 68.7 jit_solution(3626235201902238070)
XLA Ops:
  0.6 0.0 copy-start.4
  0.6 0.6 copy-done.4
  1.3 0.0 copy-start
  1.3 0.9 %copy-done = f32[16,4096]{1,0:T(8,128)S(1)} copy-done((f32[16,4096]{1,0:T(8,128)S(1)}, f32[16,4096]{1,0:T(8,128)}, u32[]{:S(2)}) %copy-start) | copy-done | bytes 262168
  2.2 0.0 copy-start.1
  2.2 0.7 %copy-done.1 = s32[4096]{0:T(1024)S(1)} copy-done((s32[4096]{0:T(1024)S(1)}, s32[4096]{0:T(1024)}, u32[]{:S(2)}) %copy-start.1) | copy-done | bytes 16408
  3.0 0.0 copy-start.2
  3.0 0.7 %copy-done.2 = s32[4096]{0:T(1024)S(1)} copy-done((s32[4096]{0:T(1024)S(1)}, s32[4096]{0:T(1024)}, u32[]{:S(2)}) %copy-start.2) | copy-done | bytes 16408
  3.7 0.3 shard_map.68
  4.0 0.0 copy-start.3
  4.0 23.4 %all_to_all.10 = f32[128,1,640]{2,1,0:T(1,128)S(1)} all-to-all(f32[128,1,640]{2,1,0:T(1,128)S(1)} %bitcast.15), channel_id=1, replica_groups=mesh['drift'=8,'cross'=16] {'drift','cross'}, dimensions={0} | all-to-all | bytes 655360 | tf_op jit(solution)/shard_map/all_to_all | solution.py:265
  27.5 0.0 copy-done.3
  27.5 24.9 %shard_map.69 = (f32[512,128]{1,0:T(8,128)S(1)}, f32[3,4096]{1,0:T(4,128)}) custom-call(f32[640,128]{1,0:T(8,128)S(1)} %bitcast.14, f32[32,128]{1,0:T(8,128)S(1)} %bitcast.21), custom_call_target="tpu_custom_call" | custom-call | tf_op jit(solution)/shard_map/pallas_call | solution.py:268
  52.4 15.3 %all_to_all.11 = f32[128,1,512]{2,1,0:T(1,128)S(1)} all-to-all(f32[128,1,512]{2,1,0:T(1,128)S(1)} %bitcast.18), channel_id=1, replica_groups=mesh['drift'=8,'cross'=16] {'drift','cross'}, dimensions={0} | all-to-all | bytes 524288 | tf_op jit(solution)/shard_map/all_to_all | solution.py:289
  67.7 1.0 %shard_map.70 = f32[2,32,8,128]{3,2,1,0:T(8,128)} custom-call(f32[512,128]{1,0:T(8,128)S(1)} %bitcast.16), custom_call_target="tpu_custom_call" | custom-call | tf_op jit(solution)/shard_map/pallas_call | solution.py:292
Async XLA Ops:
  0.6 0.7 copy-start.4
  1.3 0.9 %copy-start = (f32[16,4096]{1,0:T(8,128)S(1)}, f32[16,4096]{1,0:T(8,128)}, u32[]{:S(2)}) copy-start(f32[16,4096]{1,0:T(8,128)} %param.5) | copy-start | bytes 786436
  2.2 0.7 %copy-start.1 = (s32[4096]{0:T(1024)S(1)}, s32[4096]{0:T(1024)}, u32[]{:S(2)}) copy-start(s32[4096]{0:T(1024)} %param.7) | copy-start | bytes 49156
  3.0 0.7 %copy-start.2 = (s32[4096]{0:T(1024)S(1)}, s32[4096]{0:T(1024)}, u32[]{:S(2)}) copy-start(s32[4096]{0:T(1024)} %param.8) | copy-start | bytes 49156
  4.0 23.4 %copy-start.3 = (f32[4096]{0:T(1024)S(1)}, f32[4096]{0:T(1024)}, u32[]{:S(2)}) copy-start(f32[4096]{0:T(1024)} %param.9) | copy-start | bytes 49156

commit v2 on v1

--- a/solution.py
+++ b/solution.py
@@ -7,6 +7,7 @@
 
 CAP = 32
 MIG = 4
+GROUP = 8
 NODES = 64
 BLK_DEV = 64
 DEVS = 128
@@ -29,11 +30,23 @@
     return jnp.where(size < 0.5, near, far)
 
 
-def pack_kernel(points_ref, counts_ref, first_ref, second_ref, out_ref, counts_col):
+def pack_kernel(
+    points_hbm, counts_hbm, first_hbm, second_hbm, out_ref, points_ref, counts_ref, first_ref, second_ref, counts_col, sems
+):
+    copies = [
+        pltpu.make_async_copy(counts_hbm, counts_ref, sems.at[0]),
+        pltpu.make_async_copy(points_hbm.at[0], points_ref.at[0], sems.at[1]),
+        pltpu.make_async_copy(points_hbm.at[1], points_ref.at[1], sems.at[2]),
+        pltpu.make_async_copy(first_hbm, first_ref, sems.at[3]),
+        pltpu.make_async_copy(second_hbm, second_ref, sems.at[4]),
+    ]
+    for copy in copies:
+        copy.start()
+    lane = lax.broadcasted_iota(jnp.int32, (32, LANES), 1)
+    part = lane // CAP
+    copies[0].wait()
     counts = counts_ref[...].astype(jnp.float32)
     counts_col[...] = jnp.broadcast_to(counts, (DEVS, LANES)).T
-    lane = lax.broadcasted_iota(jnp.int32, (32, LANES), 1)
-    part = lane // CAP
 
     def feature(f):
         if f < 16:
@@ -41,6 +54,10 @@
         return (first_ref if f == 16 else second_ref)[...].astype(jnp.float32)
 
     for j in range(SEND_ROWS):
+        if j % 2 == 0:
+            copies[1 + j // 2].wait()
+        if j == 4:
+            copies[4].wait()
         rows = [feature(4 * j + ff) for ff in range(4) if 4 * j + ff < 18]
         for oo in range(4):
             block = jnp.zeros((32, LANES), jnp.float32)
@@ -55,9 +72,10 @@
             out_ref[pl.ds(SEND_ROWS * oo + j, 32, stride=4 * SEND_ROWS), :] = block
 
 
-def unpack_kernel(back_ref, out_ref):
+def unpack_kernel(back_ref, out_hbm, out_ref, sems):
     lane = lax.broadcasted_iota(jnp.int32, (32, LANES), 1)
     part = lane // CAP
+    copies = [pltpu.make_async_copy(out_ref.at[a], out_hbm.at[a], sems.at[a]) for a in range(2)]
     for j in range(BACK_ROWS):
         blocks = [back_ref[pl.ds(BACK_ROWS * oo + j, 32, stride=4 * BACK_ROWS), :] for oo in range(4)]
         for ff in range(4):
@@ -67,10 +85,14 @@
                 moved = pltpu.roll(block, ((oo - ff) * CAP) % LANES, 1) if ff != oo else block
                 row = jnp.where(part == oo, moved, row)
             out_ref[f // 8, :, f % 8, :] = row
+        if j % 2 == 1:
+            copies[j // 2].start()
+    for copy in copies:
+        copy.wait()
 
 
 def steps_kernel(
-    got_ref, contact_ref, back_ref, vel_ref, state, terms, patterns, sums, selector, parts, reduced, keep, pairs
+    got_ref, contact_ref, back_ref, vel_hbm, state, terms, patterns, sums, selector, parts, reduced, keep, pairs, vel, sem
 ):
     def rows_of(f):
         return state[f * CAP : (f + 1) * CAP, :]
@@ -93,7 +115,7 @@
     block_of = lax.broadcasted_iota(jnp.int32, (BLK_DEV, LANES), 0).astype(jnp.float32)
     half = lax.broadcasted_iota(jnp.int32, (3 * NODES, LANES), 1) < BLK_DEV
 
-    def one_step(ids_row):
+    def one_step(ids_row, when_node=None):
         position = [rows_of(e) for e in range(3)]
         velocity = [rows_of(3 + c) for c in range(3)]
         affine = [[rows_of(6 + 3 * c + e) for e in range(3)] for c in range(3)]
@@ -126,7 +148,7 @@
 
         sums[...] = jnp.zeros_like(sums)
 
-        def scatter(c, unused):
+        def scatter_operands(c):
             ids = state[pl.ds(ids_row * CAP + c, 1), :]
             chosen = jnp.where(block_of == ids, 1.0, 0.0).astype(jnp.bfloat16)
             selector[c] = chosen
@@ -146,15 +168,23 @@
             high = full.astype(jnp.bfloat16)
             low = (full - high.astype(jnp.float32)).astype(jnp.bfloat16)
             twice = jnp.concatenate([chosen, chosen], axis=0)
+            return [high, low], [twice, twice]
+
+        def scatter(step, unused):
+            values, selectors = [], []
+            for u in range(GROUP):
+                a, b = scatter_operands(GROUP * step + u)
+                values += a
+                selectors += b
             sums[...] += lax.dot_general(
-                jnp.concatenate([high, low], axis=1),
-                jnp.concatenate([twice, twice], axis=1),
+                jnp.concatenate(values, axis=1),
+                jnp.concatenate(selectors, axis=1),
                 (((1,), (1,)), ((), ())),
                 preferred_element_type=jnp.float32,
             )
             return unused
 
-        lax.fori_loop(0, CAP, scatter, 0)
+        lax.fori_loop(0, CAP // GROUP, scatter, 0, unroll=2)
 
         grid_mass = jnp.maximum(sums[0:NODES, :], 0.5)
         node = []
@@ -163,6 +193,8 @@
             if v == 2:
                 value = value - STEP_DURATION * GRAVITY_ACCEL
             node.append(value * keep[...])
+        if when_node is not None:
+            when_node(node)
         whole = jnp.concatenate(node, axis=0)
         first = whole.astype(jnp.bfloat16).astype(jnp.float32)
         rest = whole - first
@@ -171,29 +203,32 @@
         parts[:, 0:LANES] = jnp.where(half, first, second).astype(jnp.bfloat16)
         parts[:, LANES : 2 * LANES] = third.astype(jnp.bfloat16)
 
-        def gather(c, unused):
-            chosen = selector[c]
-            nodal = jnp.dot(
+        def gather(step, unused):
+            chosen = jnp.concatenate([selector[GROUP * step + u] for u in range(GROUP)], axis=1)
+            nodal_all = jnp.dot(
                 parts[...],
                 jnp.concatenate([chosen, chosen, chosen, chosen], axis=0),
                 preferred_element_type=jnp.float32,
             )
-            inner = pair_weights(c)
-            weights = [term(13 + i, c) * inner[h] for i in range(4) for h in range(2)]
-            for v in range(3):
-                weighted = [
-                    weights[n] * nodal[v * NODES + 8 * n : v * NODES + 8 * (n + 1), :] for n in range(8)
-                ]
-                by_i = [weighted[2 * i] + weighted[2 * i + 1] for i in range(4)]
-                odd = (weighted[1] + weighted[3]) + (weighted[5] + weighted[7])
-                outer = by_i[2] + by_i[3]
-                total = (by_i[0] + by_i[1]) + outer
-                first_moment = (by_i[1] + by_i[3]) + (outer + outer)
-                for t, value in enumerate((total, odd, first_moment)):
-                    reduced[pl.ds((3 * v + t) * 8 * CAP + c * 8, 8), :] = value
+            for u in range(GROUP):
+                c = GROUP * step + u
+                nodal = nodal_all[:, u * LANES : (u + 1) * LANES]
+                inner = pair_weights(c)
+                weights = [term(13 + i, c) * inner[h] for i in range(4) for h in range(2)]
+                for v in range(3):
+                    weighted = [
+                        weights[n] * nodal[v * NODES + 8 * n : v * NODES + 8 * (n + 1), :] for n in range(8)
+                    ]
+                    by_i = [weighted[2 * i] + weighted[2 * i + 1] for i in range(4)]
+                    odd = (weighted[1] + weighted[3]) + (weighted[5] + weighted[7])
+                    outer = by_i[2] + by_i[3]
+                    total = (by_i[0] + by_i[1]) + outer
+                    first_moment = (by_i[1] + by_i[3]) + (outer + outer)
+                    for t, value in enumerate((total, odd, first_moment)):
+                        reduced[pl.ds((3 * v + t) * 8 * CAP + c * 8, 8), :] = value
             return unused
 
-        lax.fori_loop(0, CAP, gather, 0)
+        lax.fori_loop(0, CAP // GROUP, gather, 0, unroll=2)
 
         def spread(v, t):
             return [reduced[pl.ds((3 * v + t) * 8 * CAP + r, CAP, stride=8), :] for r in range(8)]
@@ -220,7 +255,6 @@
             put(3 + v, jnp.where(alive, new_velocity, velocity[v]))
             new_position = jnp.clip(position[v] + STEP_DURATION * new_velocity, 0.5, 2.5)
             put(v, jnp.where(alive, new_position, position[v]))
-        return node
 
     one_step(16)
 
@@ -234,34 +268,52 @@
         )
         state[at : at + 2 * MIG, :] = jnp.where(slot < MIG, across, pltpu.roll(old, N_CROSS, 1))
 
-    node = one_step(17)
+    copy = pltpu.make_async_copy(vel, vel_hbm, sem)
+
+    def send_velocity(node):
+        lane = lax.broadcasted_iota(jnp.int32, (32, LANES), 1)
+        for v in range(3):
+            pairs[...] = jnp.concatenate([node[v], node[v]], axis=0).T[0:BLK_DEV, :]
+            packed = jnp.where(lane < NODES, pairs[pl.ds(0, 32, stride=2), :], pairs[pl.ds(1, 32, stride=2), :])
+            for q in range(32):
+                vel[v : v + 1, q * LANES : (q + 1) * LANES] = packed[q : q + 1, :]
+        copy.start()
+
+    one_step(17, send_velocity)
 
     for j in range(BACK_ROWS):
         back_ref[pl.ds(j, DEVS, stride=BACK_ROWS), :] = state[j * LANES : (j + 1) * LANES, :].T
 
-    lane = lax.broadcasted_iota(jnp.int32, (32, LANES), 1)
-    for v in range(3):
-        pairs[...] = jnp.concatenate([node[v], node[v]], axis=0).T[0:BLK_DEV, :]
-        packed = jnp.where(lane < NODES, pairs[pl.ds(0, 32, stride=2), :], pairs[pl.ds(1, 32, stride=2), :])
-        for q in range(32):
-            vel_ref[v : v + 1, q * LANES : (q + 1) * LANES] = packed[q : q + 1, :]
+    copy.wait()
 
 
 def in_vmem(count):
     return [pl.BlockSpec(memory_space=pltpu.VMEM)] * count
+
+
+def in_hbm(count):
+    return [pl.BlockSpec(memory_space=pltpu.HBM)] * count
 
 
 def local(points, send_counts, block_first, block_second, contact):
     params = pltpu.CompilerParams(vmem_limit_bytes=VMEM_LIMIT)
     tiled = points.reshape(2, 8, 32, LANES).transpose(0, 2, 1, 3)
+    operands = (tiled, send_counts.reshape(1, DEVS), block_first.reshape(32, LANES), block_second.reshape(32, LANES))
     send = pl.pallas_call(
         pack_kernel,
         out_shape=jax.ShapeDtypeStruct((DEVS * SEND_ROWS, LANES), jnp.float32),
-        in_specs=in_vmem(4),
+        in_specs=in_hbm(4),
         out_specs=in_vmem(1)[0],
-        scratch_shapes=[pltpu.VMEM((DEVS, LANES), jnp.float32)],
+        scratch_shapes=[
+            pltpu.VMEM((2, 32, 8, LANES), jnp.float32),
+            pltpu.VMEM((1, DEVS), jnp.int32),
+            pltpu.VMEM((32, LANES), jnp.int32),
+            pltpu.VMEM((32, LANES), jnp.int32),
+            pltpu.VMEM((DEVS, LANES), jnp.float32),
+            pltpu.SemaphoreType.DMA((5,)),
+        ],
         compiler_params=params,
-    )(tiled, send_counts.reshape(1, DEVS), block_first.reshape(32, LANES), block_second.reshape(32, LANES))
+    )(*(pltpu.with_memory_space_constraint(value, pltpu.HBM) for value in operands))
     got = lax.all_to_all(
         send.reshape(DEVS, 1, SEND_ROWS * LANES), ("drift", "cross"), split_axis=0, concat_axis=0, tiled=True
     )
@@ -272,7 +324,7 @@
             jax.ShapeDtypeStruct((3, BLK_DEV * NODES), jnp.float32),
         ),
         in_specs=in_vmem(2),
-        out_specs=tuple(in_vmem(2)),
+        out_specs=(in_vmem(1)[0], in_hbm(1)[0]),
         scratch_shapes=[
             pltpu.VMEM((SEND_ROWS * LANES, LANES), jnp.float32),
             pltpu.VMEM((17 * CAP, LANES), jnp.float32),
@@ -283,6 +335,8 @@
             pltpu.VMEM((9 * 8 * CAP, LANES), jnp.float32),
             pltpu.VMEM((NODES, LANES), jnp.float32),
             pltpu.VMEM((BLK_DEV, LANES), jnp.float32),
+            pltpu.VMEM((3, BLK_DEV * NODES), jnp.float32),
+            pltpu.SemaphoreType.DMA(()),
         ],
         compiler_params=params,
     )(got.reshape(DEVS * SEND_ROWS, LANES), contact.reshape(32, LANES))
@@ -293,7 +347,8 @@
         unpack_kernel,
         out_shape=jax.ShapeDtypeStruct((2, 32, 8, LANES), jnp.float32),
         in_specs=in_vmem(1),
-        out_specs=in_vmem(1)[0],
+        out_specs=in_hbm(1)[0],
+        scratch_shapes=[pltpu.VMEM((2, 32, 8, LANES), jnp.float32), pltpu.SemaphoreType.DMA((2,))],
         compiler_params=params,
     )(returned.reshape(DEVS * BACK_ROWS, LANES))
     return (final.transpose(0, 2, 1, 3).reshape(16, DEVS * CAP), node_velocity)

time: 69 us -> 47.5 us (0.69)
  Pallas kernels: 26.3 us -> 7.92 us
  local copies, waits for them, and re-layouts: 3.04 us -> 0.01 us
    pallas_call x1, Pallas kernels: 24.9 us -> 5.48 us  [local(): pl.pallas_call(steps_kernel, out_shape=(jax.ShapeDtypeStruct((DEVS * BACK...]
    unnamed x10 -> x2, local copies, waits for them, and re-layouts: 3.04 us -> 0.01 us
    pallas_call x1, Pallas kernels: 0.32 us -> 1.44 us  [local(): pl.pallas_call(pack_kernel, out_shape=jax.ShapeDtypeStruct((DEVS * SEND_R...]
where the time goes in v2:
time: 47.5 us; the launch traced here: 47.3 us
  blocking collectives  38.7 us (81%)
  Pallas kernels  7.92 us (17%)
  between operations  0.66 us (1%)
    all_to_all x1, blocking collectives, local(): lax.all_to_all(send.reshape(DEVS, 1, SEND_ROWS * LANES), ('drift', 'cross...  23.4 us
    all_to_all x1, blocking collectives, local(): lax.all_to_all(back.reshape(DEVS, 1, BACK_ROWS * LANES), ('drift', 'cross...  15.3 us
    pallas_call x1, Pallas kernels, local(): pl.pallas_call(steps_kernel, out_shape=(jax.ShapeDtypeStruct((DEVS * BACK...  5.48 us
    pallas_call x1, Pallas kernels, local(): pl.pallas_call(pack_kernel, out_shape=jax.ShapeDtypeStruct((DEVS * SEND_R...  1.44 us
    pallas_call x1, Pallas kernels, local(): pl.pallas_call(unpack_kernel, out_shape=jax.ShapeDtypeStruct((2, 32, 8, L...  0.99 us

profile of v2, /device:TPU:1, one launch (start us, length us, event | category | flops | bytes accessed | tf_op | source)
XLA Modules:
  0.0 47.3 jit_solution(3852539021726820393)
XLA Ops:
  0.6 1.4 %shard_map.68 = f32[640,128]{1,0:T(8,128)S(1)} custom-call(f32[2,32,8,128]{3,2,1,0:T(8,128)} %bitcast.19, s32[1,128]{1,0:T(1,128)} %bitcast.23, s32[32,128]{1,0:T(8,128)} %bitcast.21, s32[32,128]{1,0:T(8,128)} %bitcast.22), custom_call_target="tpu_custom_call" | custom-call | tf_op jit(solution)/shard_map/pallas_call | solution.py:302
  2.1 0.0 copy-start
  2.1 23.4 %all_to_all.10 = f32[128,1,640]{2,1,0:T(1,128)S(1)} all-to-all(f32[128,1,640]{2,1,0:T(1,128)S(1)} %bitcast.15), channel_id=1, replica_groups=mesh['drift'=8,'cross'=16] {'drift','cross'}, dimensions={0} | all-to-all | bytes 655360 | tf_op jit(solution)/shard_map/all_to_all | solution.py:317
  25.5 0.0 copy-done
  25.5 5.5 %shard_map.69 = (f32[512,128]{1,0:T(8,128)S(1)}, f32[3,4096]{1,0:T(4,128)}) custom-call(f32[640,128]{1,0:T(8,128)S(1)} %bitcast.14, f32[32,128]{1,0:T(8,128)S(1)} %bitcast.18), custom_call_target="tpu_custom_call" | custom-call | tf_op jit(solution)/shard_map/pallas_call | solution.py:320
  31.0 15.3 %all_to_all.11 = f32[128,1,512]{2,1,0:T(1,128)S(1)} all-to-all(f32[128,1,512]{2,1,0:T(1,128)S(1)} %bitcast.17), channel_id=1, replica_groups=mesh['drift'=8,'cross'=16] {'drift','cross'}, dimensions={0} | all-to-all | bytes 524288 | tf_op jit(solution)/shard_map/all_to_all | solution.py:343
  46.3 1.0 %shard_map.70 = f32[2,32,8,128]{3,2,1,0:T(8,128)} custom-call(f32[512,128]{1,0:T(8,128)S(1)} %bitcast.16), custom_call_target="tpu_custom_call" | custom-call | tf_op jit(solution)/shard_map/pallas_call | solution.py:346
Async XLA Ops:
  2.1 23.4 %copy-start = (f32[4096]{0:T(1024)S(1)}, f32[4096]{0:T(1024)}, u32[]{:S(2)}) copy-start(f32[4096]{0:T(1024)} %param.9) | copy-start | bytes 49156

commit v3 on v2

v3 whole, which is shorter than its diff:
```python
import jax
import jax.numpy as jnp
from jax import lax
from jax.experimental import pallas as pl
from jax.experimental.pallas import tpu as pltpu
from jax.sharding import PartitionSpec as P

CAP = 32
MIG = 4
NODES = 64
BLK_DEV = 64
DEVS = 128
N_CROSS = 16
LANES = 128

STEP_DURATION = 0.1
GRAVITY_ACCEL = 1.0

SEND_ROWS = 5
BACK_ROWS = 4

UNPACK_PARTS = 2

ROW = 23
SLOT = 3

VMEM_LIMIT = 32 * 1024 * 1024


def spline(dist):
    size = jnp.abs(dist)
    near = 0.75 - size * size
    far = 0.5 * jnp.square(jnp.maximum(1.5 - size, 0.0))
    return jnp.where(size < 0.5, near, far)


def pack_kernel(
    points_hbm, counts_hbm, first_hbm, second_hbm, out_ref, points_ref, counts_ref, first_ref, second_ref, counts_col, sems
):
    moves = ((counts_hbm, counts_ref), (points_hbm, points_ref), (first_hbm, first_ref), (second_hbm, second_ref))
    copies = [pltpu.make_async_copy(source, target, sems.at[n]) for n, (source, target) in enumerate(moves)]
    for copy in copies:
        copy.start()
    lane = lax.broadcasted_iota(jnp.int32, (32, LANES), 1)
    quarter = lane // CAP
    slot = (lane - 3 * CAP).astype(jnp.float32)
    copies[0].wait()
    counts = counts_ref[...].astype(jnp.float32)
    counts_col[...] = jnp.broadcast_to(counts, (DEVS, LANES)).T
    for copy in copies[1:]:
        copy.wait()

    def feature(f):
        if f < 16:
            return points_ref[f // 8, :, f % 8, :]
        return (first_ref if f == 16 else second_ref)[...].astype(jnp.float32)

    for j in range(SEND_ROWS):
        rows = [feature(4 * j + ff) for ff in range(4) if 4 * j + ff < 18]
        for oo in range(4):
            block = jnp.zeros((32, LANES), jnp.float32)
            for ff, row in enumerate(rows):
                moved = pltpu.roll(row, ((ff - oo) * CAP) % LANES, 1) if ff != oo else row
                block = jnp.where(quarter == ff, moved, block)
            if j == 3:
                count = counts_col[pl.ds(oo, 32, stride=4), :]
                live = (slot < count).astype(jnp.float32)
                block = jnp.where(quarter == 3, block * live, block)
            out_ref[pl.ds(SEND_ROWS * oo + j, 32, stride=4 * SEND_ROWS), :] = block


def unpack_kernel(back_ref, out_hbm, out_ref, sems):
    tiles = 32 // UNPACK_PARTS
    lane = lax.broadcasted_iota(jnp.int32, (tiles, LANES), 1)
    quarter = lane // CAP
    copies = []
    for part in range(UNPACK_PARTS):
        at = slice(tiles * part, tiles * (part + 1))
        for j in range(BACK_ROWS):
            from_row = 4 * BACK_ROWS * tiles * part + j
            blocks = [back_ref[pl.ds(from_row + BACK_ROWS * oo, tiles, stride=4 * BACK_ROWS), :] for oo in range(4)]
            for ff in range(4):
                f = 4 * j + ff
                row = blocks[0]
                for oo, block in enumerate(blocks):
                    moved = pltpu.roll(block, ((oo - ff) * CAP) % LANES, 1) if ff != oo else block
                    row = jnp.where(quarter == oo, moved, row)
                out_ref[f // 8, at, f % 8, :] = row
        piece = pl.ds(tiles * part, tiles)
        copies.append(pltpu.make_async_copy(out_ref.at[:, piece], out_hbm.at[:, piece], sems.at[part]))
        copies[-1].start()
    for copy in copies:
        copy.wait()


def steps_kernel(
    got_ref,
    contact_ref,
    back_ref,
    vel_hbm,
    state,
    cells,
    values,
    weights,
    sums,
    nodes,
    parts,
    reduced,
    keep,
    pairs,
    vel,
    sem,
):
    def rows_of(f):
        return state[f * CAP : (f + 1) * CAP, :]

    def put(f, value):
        state[f * CAP : (f + 1) * CAP, :] = value

    for j in range(SEND_ROWS):
        state[j * LANES : (j + 1) * LANES, :] = got_ref[pl.ds(j, DEVS, stride=SEND_ROWS), :].T

    contact = contact_ref[...]
    pairs[pl.ds(0, 32, stride=2), :] = contact
    pairs[pl.ds(1, 32, stride=2), :] = pltpu.roll(contact, NODES, 1)
    turned = jnp.concatenate([pairs[...], pairs[...]], axis=0).T
    keep[...] = 1.0 - turned[0:NODES, :]

    def half(rows):
        return lax.broadcasted_iota(jnp.int32, (rows, LANES), 1) < BLK_DEV

    def numbers(rows):
        return lax.broadcasted_iota(jnp.int32, (rows, LANES), 0).astype(jnp.float32)

    def chosen(row, rows):
        return jnp.where(numbers(rows) == row, 1.0, 0.0).astype(jnp.bfloat16)

    sub = lax.broadcasted_iota(jnp.int32, (8, LANES), 0)
    k_of = (sub % 4).astype(jnp.float32)
    j_of = (sub // 4).astype(jnp.float32)

    def one_step(ids_row, when_node=None):
        sums[...] = jnp.zeros_like(sums)

        def scatter(group, unused):
            def feature(f):
                return state[pl.ds(pl.multiple_of(f * CAP + 8 * group, 8), 8), :]

            position = [feature(e) for e in range(3)]
            mass = feature(15)
            cell = jnp.where(position[0] >= 1.5, 1.0, 0.0)
            within = position[0] - cell
            at_cells = pl.ds(pl.multiple_of(8 * group, 8), 8)
            cells[at_cells, :] = feature(ids_row) + BLK_DEV * cell
            first = [spline(within - float(o)) for o in range(3)]
            second = [spline(position[1] - float(j)) for j in range(4)]
            third = [spline(position[2] - float(k)) for k in range(4)]
            for o in range(3):
                for j in range(4):
                    product = first[o] * second[j]
                    for k in range(4):
                        r = 16 * o + 4 * j + k
                        weights[group, pl.ds(ROW * r, 8, stride=SLOT), :] = product * third[k]

            def write(q, value):
                values[group, 8 * q : 8 * q + 8, :] = value

            write(0, mass)
            for v in range(3):
                along = [feature(6 + 3 * v + e) for e in range(3)]
                moved = along[0] * within + along[1] * position[1] + along[2] * position[2]
                write(1 + v, feature(3 + v) - moved)
                for e in range(3):
                    write(4 + 3 * v + e, along[e])

            terms, selectors = [], []
            for u in range(8):

                def term(q):
                    return values[group, 8 * q + u : 8 * q + u + 1, :]

                weight = weights[group, pl.ds(SLOT * u, 48, stride=ROW), :]
                heavy = [weight[8 * n : 8 * n + 8] * term(0) for n in range(6)]
                pieces = list(heavy)
                for v in range(3):
                    start = term(1 + v) + term(6 + 3 * v) * k_of
                    along = term(4 + 3 * v)
                    at = [start + term(5 + 3 * v) * j_of, start + term(5 + 3 * v) * (j_of + 2.0)]
                    for o in range(3):
                        pieces += [heavy[2 * o + h] * at[h] for h in range(2)]
                        at = [a + along for a in at]
                full = jnp.concatenate(pieces, axis=0)
                high = full.astype(jnp.bfloat16)
                low = (full - high.astype(jnp.float32)).astype(jnp.bfloat16)
                one = chosen(cells[pl.ds(8 * group + u, 1), :], 2 * BLK_DEV)
                terms += [high, low]
                selectors += [one, one]
            sums[...] += lax.dot_general(
                jnp.concatenate(terms, axis=1),
                jnp.concatenate(selectors, axis=1),
                (((1,), (1,)), ((), ())),
                preferred_element_type=jnp.float32,
            )
            return unused

        lax.fori_loop(0, CAP // 8, scatter, 0, unroll=4)

        low_half = half(16)
        for f in range(4):
            lower = [sums[48 * f + 16 * o : 48 * f + 16 * o + 16, :] for o in range(3)]
            other = [pltpu.roll(value, BLK_DEV, 1) for value in lower]
            for i in range(4):
                total = None
                if i < 3:
                    total = jnp.where(low_half, lower[i], other[i])
                if i > 0:
                    moved = jnp.where(low_half, other[i - 1], lower[i - 1])
                    total = moved if total is None else total + moved
                nodes[64 * f + 16 * i : 64 * f + 16 * i + 16, :] = total

        grid_mass = jnp.maximum(nodes[0:NODES, :], 0.5)
        node = []
        for v in range(3):
            value = nodes[(1 + v) * NODES : (2 + v) * NODES, :] / grid_mass
            if v == 2:
                value = value - STEP_DURATION * GRAVITY_ACCEL
            node.append(value * keep[...])
        if when_node is not None:
            when_node(node)
        for v in range(3):
            for o in range(3):
                value = jnp.where(low_half, node[v][16 * o : 16 * o + 16], node[v][16 * o + 16 : 16 * o + 32])
                high = value.astype(jnp.bfloat16)
                low = (value - high.astype(jnp.float32)).astype(jnp.bfloat16)
                at = 48 * v + 16 * o
                parts[at : at + 16, 0:LANES] = high
                parts[at : at + 16, LANES : 2 * LANES] = low

        def gather(group, unused):
            slots = [8 * group + u for u in range(8)]
            selectors = [chosen(cells[pl.ds(c, 1), :], 2 * BLK_DEV) for c in slots]
            selector = jnp.concatenate(selectors, axis=1)
            nodal_all = jnp.dot(
                parts[...], jnp.concatenate([selector, selector], axis=0), preferred_element_type=jnp.float32
            )
            for u, c in enumerate(slots):
                weight = weights[c // 8, pl.ds(SLOT * (c % 8), 48, stride=ROW), :]
                for v in range(3):
                    nodal = nodal_all[48 * v : 48 * (v + 1), u * LANES : (u + 1) * LANES]
                    weighted = [weight[8 * n : 8 * n + 8] * nodal[8 * n : 8 * n + 8] for n in range(6)]
                    by_i = [weighted[2 * o] + weighted[2 * o + 1] for o in range(3)]
                    odd = (weighted[1] + weighted[3]) + weighted[5]
                    outer = by_i[1] + by_i[2]
                    for t, value in enumerate((by_i[0] + outer, odd, outer + by_i[2])):
                        reduced[3 * v + t, pl.ds(ROW * c, 8, stride=SLOT), :] = value
            return unused

        lax.fori_loop(0, CAP // 8, gather, 0, unroll=2)

        def spread(v, t):
            return [reduced[3 * v + t, pl.ds(SLOT * r, CAP, stride=ROW), :] for r in range(8)]

        def add_all(terms):
            total = terms[0]
            for term in terms[1:]:
                total = total + term
            return total

        position = [rows_of(e) for e in range(3)]
        centre = [position[0] - jnp.where(position[0] >= 1.5, 1.0, 0.0), position[1], position[2]]
        alive = rows_of(15) > 0.0
        for v in range(3):
            by_row = spread(v, 0)
            by_k = [by_row[k] + by_row[4 + k] for k in range(4)]
            new_velocity = (by_k[0] + by_k[1]) + (by_k[2] + by_k[3])
            moment = [
                add_all(spread(v, 2)),
                2.0 * add_all(spread(v, 1)) + add_all(by_row[4:]),
                (by_k[1] + by_k[3]) + 2.0 * (by_k[2] + by_k[3]),
            ]
            for e in range(3):
                new_affine = 4.0 * (moment[e] - centre[e] * new_velocity)
                put(6 + 3 * v + e, jnp.where(alive, new_affine, rows_of(6 + 3 * v + e)))
            put(3 + v, jnp.where(alive, new_velocity, rows_of(3 + v)))
            new_position = jnp.clip(position[v] + STEP_DURATION * new_velocity, 0.5, 2.5)
            put(v, jnp.where(alive, new_position, position[v]))

    one_step(16)

    source = lax.broadcasted_iota(jnp.int32, (2 * MIG, LANES), 1)
    slot = lax.broadcasted_iota(jnp.int32, (2 * MIG, LANES), 0)
    for f in range(16):
        at = f * CAP + CAP - 2 * MIG
        old = state[at : at + 2 * MIG, :]
        across = jnp.where(
            source % N_CROSS == 0, pltpu.roll(old, LANES - (N_CROSS - 1), 1), pltpu.roll(old, 1, 1)
        )
        state[at : at + 2 * MIG, :] = jnp.where(slot < MIG, across, pltpu.roll(old, N_CROSS, 1))

    copy = pltpu.make_async_copy(vel, vel_hbm, sem)

    def send_velocity(node):
        lane = lax.broadcasted_iota(jnp.int32, (32, LANES), 1)
        for v in range(3):
            pairs[...] = jnp.concatenate([node[v], node[v]], axis=0).T[0:BLK_DEV, :]
            packed = jnp.where(lane < NODES, pairs[pl.ds(0, 32, stride=2), :], pairs[pl.ds(1, 32, stride=2), :])
            for q in range(32):
                vel[v : v + 1, q * LANES : (q + 1) * LANES] = packed[q : q + 1, :]
        copy.start()

    one_step(17, send_velocity)

    for j in range(BACK_ROWS):
        back_ref[pl.ds(j, DEVS, stride=BACK_ROWS), :] = state[j * LANES : (j + 1) * LANES, :].T

    copy.wait()


def in_vmem(count):
    return [pl.BlockSpec(memory_space=pltpu.VMEM)] * count


def in_hbm(count):
    return [pl.BlockSpec(memory_space=pltpu.HBM)] * count


def local(points, send_counts, block_first, block_second, contact):
    params = pltpu.CompilerParams(vmem_limit_bytes=VMEM_LIMIT)
    tiled = points.reshape(2, 8, 32, LANES).transpose(0, 2, 1, 3)
    operands = (tiled, send_counts.reshape(1, DEVS), block_first.reshape(32, LANES), block_second.reshape(32, LANES))
    send = pl.pallas_call(
        pack_kernel,
        out_shape=jax.ShapeDtypeStruct((DEVS * SEND_ROWS, LANES), jnp.float32),
        in_specs=in_hbm(4),
        out_specs=in_vmem(1)[0],
        scratch_shapes=[
            pltpu.VMEM((2, 32, 8, LANES), jnp.float32),
            pltpu.VMEM((1, DEVS), jnp.int32),
            pltpu.VMEM((32, LANES), jnp.int32),
            pltpu.VMEM((32, LANES), jnp.int32),
            pltpu.VMEM((DEVS, LANES), jnp.float32),
            pltpu.SemaphoreType.DMA((4,)),
        ],
        compiler_params=params,
    )(*(pltpu.with_memory_space_constraint(value, pltpu.HBM) for value in operands))
    got = lax.all_to_all(
        send.reshape(DEVS, 1, SEND_ROWS * LANES), ("drift", "cross"), split_axis=0, concat_axis=0, tiled=True
    )
    back, node_velocity = pl.pallas_call(
        steps_kernel,
        out_shape=(
            jax.ShapeDtypeStruct((DEVS * BACK_ROWS, LANES), jnp.float32),
            jax.ShapeDtypeStruct((3, BLK_DEV * NODES), jnp.float32),
        ),
        in_specs=in_vmem(2),
        out_specs=(in_vmem(1)[0], in_hbm(1)[0]),
        scratch_shapes=[
            pltpu.VMEM((SEND_ROWS * LANES, LANES), jnp.float32),
            pltpu.VMEM((CAP, LANES), jnp.float32),
            pltpu.VMEM((CAP // 8, 13 * 8, LANES), jnp.float32),
            pltpu.VMEM((CAP // 8, 48 * ROW, LANES), jnp.float32),
            pltpu.VMEM((192, 2 * BLK_DEV), jnp.float32),
            pltpu.VMEM((4 * NODES, LANES), jnp.float32),
            pltpu.VMEM((144, 2 * LANES), jnp.bfloat16),
            pltpu.VMEM((9, ROW * CAP, LANES), jnp.float32),
            pltpu.VMEM((NODES, LANES), jnp.float32),
            pltpu.VMEM((BLK_DEV, LANES), jnp.float32),
            pltpu.VMEM((3, BLK_DEV * NODES), jnp.float32),
            pltpu.SemaphoreType.DMA(()),
        ],
        compiler_params=params,
    )(got.reshape(DEVS * SEND_ROWS, LANES), contact.reshape(32, LANES))
    returned = lax.all_to_all(
        back.reshape(DEVS, 1, BACK_ROWS * LANES), ("drift", "cross"), split_axis=0, concat_axis=0, tiled=True
    )
    final = pl.pallas_call(
        unpack_kernel,
        out_shape=jax.ShapeDtypeStruct((2, 32, 8, LANES), jnp.float32),
        in_specs=in_vmem(1),
        out_specs=in_hbm(1)[0],
        scratch_shapes=[pltpu.VMEM((2, 32, 8, LANES), jnp.float32), pltpu.SemaphoreType.DMA((UNPACK_PARTS,))],
        compiler_params=params,
    )(returned.reshape(DEVS * BACK_ROWS, LANES))
    return (final.transpose(0, 2, 1, 3).reshape(16, DEVS * CAP), node_velocity)


def solution(mesh):
    return jax.shard_map(
        local,
        mesh=mesh,
        in_specs=(
            P(None, ("drift", "cross")),
            P(("drift", "cross")),
            P(("drift", "cross")),
            P(("drift", "cross")),
            P(("drift", "cross")),
        ),
        out_specs=(P(None, ("drift", "cross")), P(None, ("drift", "cross"))),
        check_vma=False,
    )
```

time: 47.5 us -> 46 us (0.968)
  Pallas kernels: 7.92 us -> 6.44 us
    pallas_call x1, Pallas kernels: 5.48 us -> 4.15 us  [local(): pl.pallas_call(steps_kernel, out_shape=(jax.ShapeDtypeStruct((DEVS * BACK...]
where the time goes in v3:
time: 46 us; the launch traced here: 45.8 us
  blocking collectives  38.7 us (84%)
  Pallas kernels  6.44 us (14%)
  between operations  0.66 us (1%)
    all_to_all x1, blocking collectives, local(): lax.all_to_all(send.reshape(DEVS, 1, SEND_ROWS * LANES), ('drift', 'cross...  23.4 us
    all_to_all x1, blocking collectives, local(): lax.all_to_all(back.reshape(DEVS, 1, BACK_ROWS * LANES), ('drift', 'cross...  15.3 us
    pallas_call x1, Pallas kernels, local(): pl.pallas_call(steps_kernel, out_shape=(jax.ShapeDtypeStruct((DEVS * BACK...  4.15 us
    pallas_call x1, Pallas kernels, local(): pl.pallas_call(pack_kernel, out_shape=jax.ShapeDtypeStruct((DEVS * SEND_R...  1.32 us
    pallas_call x1, Pallas kernels, local(): pl.pallas_call(unpack_kernel, out_shape=jax.ShapeDtypeStruct((2, 32, 8, L...  0.98 us

profile of v3, /device:TPU:1, one launch (start us, length us, event | category | flops | bytes accessed | tf_op | source)
XLA Modules:
  0.0 45.8 jit_solution(18181527005761892889)
XLA Ops:
  0.6 1.3 %shard_map.68 = f32[640,128]{1,0:T(8,128)S(1)} custom-call(f32[2,32,8,128]{3,2,1,0:T(8,128)} %bitcast.19, s32[1,128]{1,0:T(1,128)} %bitcast.23, s32[32,128]{1,0:T(8,128)} %bitcast.21, s32[32,128]{1,0:T(8,128)} %bitcast.22), custom_call_target="tpu_custom_call" | custom-call | tf_op jit(solution)/shard_map/pallas_call | solution.py:331
  2.0 0.0 copy-start
  2.0 23.4 %all_to_all.10 = f32[128,1,640]{2,1,0:T(1,128)S(1)} all-to-all(f32[128,1,640]{2,1,0:T(1,128)S(1)} %bitcast.15), channel_id=1, replica_groups=mesh['drift'=8,'cross'=16] {'drift','cross'}, dimensions={0} | all-to-all | bytes 655360 | tf_op jit(solution)/shard_map/all_to_all | solution.py:346
  25.4 0.0 copy-done
  25.4 4.1 %shard_map.69 = (f32[512,128]{1,0:T(8,128)S(1)}, f32[3,4096]{1,0:T(4,128)}) custom-call(f32[640,128]{1,0:T(8,128)S(1)} %bitcast.14, f32[32,128]{1,0:T(8,128)S(1)} %bitcast.18), custom_call_target="tpu_custom_call" | custom-call | tf_op jit(solution)/shard_map/pallas_call | solution.py:349
  29.6 15.3 %all_to_all.11 = f32[128,1,512]{2,1,0:T(1,128)S(1)} all-to-all(f32[128,1,512]{2,1,0:T(1,128)S(1)} %bitcast.17), channel_id=1, replica_groups=mesh['drift'=8,'cross'=16] {'drift','cross'}, dimensions={0} | all-to-all | bytes 524288 | tf_op jit(solution)/shard_map/all_to_all | solution.py:373
  44.8 1.0 %shard_map.70 = f32[2,32,8,128]{3,2,1,0:T(8,128)} custom-call(f32[512,128]{1,0:T(8,128)S(1)} %bitcast.16), custom_call_target="tpu_custom_call" | custom-call | tf_op jit(solution)/shard_map/pallas_call | solution.py:376
Async XLA Ops:
  2.0 23.4 %copy-start = (f32[4096]{0:T(1024)S(1)}, f32[4096]{0:T(1024)}, u32[]{:S(2)}) copy-start(f32[4096]{0:T(1024)} %param.9) | copy-start | bytes 49156

commit v4 on v3

--- a/solution.py
+++ b/solution.py
@@ -19,7 +19,7 @@
 SEND_ROWS = 5
 BACK_ROWS = 4
 
-UNPACK_PARTS = 2
+UNPACK_PARTS = 4
 
 ROW = 23
 SLOT = 3
@@ -32,6 +32,22 @@
     near = 0.75 - size * size
     far = 0.5 * jnp.square(jnp.maximum(1.5 - size, 0.0))
     return jnp.where(size < 0.5, near, far)
+
+
+def exchange_quarters(rows, quarter):
+    turned = []
+    for d in range(4):
+        mixed = rows[d]
+        for q in range(1, 4):
+            mixed = jnp.where(quarter == q, rows[(q + d) % 4], mixed)
+        turned.append(pltpu.roll(mixed, d * CAP, 1) if d else mixed)
+    result = []
+    for q in range(4):
+        mixed = turned[-q % 4]
+        for p in range(1, 4):
+            mixed = jnp.where(quarter == p, turned[(p - q) % 4], mixed)
+        result.append(mixed)
+    return result
 
 
 def pack_kernel(
@@ -56,12 +72,8 @@
         return (first_ref if f == 16 else second_ref)[...].astype(jnp.float32)
 
     for j in range(SEND_ROWS):
-        rows = [feature(4 * j + ff) for ff in range(4) if 4 * j + ff < 18]
-        for oo in range(4):
-            block = jnp.zeros((32, LANES), jnp.float32)
-            for ff, row in enumerate(rows):
-                moved = pltpu.roll(row, ((ff - oo) * CAP) % LANES, 1) if ff != oo else row
-                block = jnp.where(quarter == ff, moved, block)
+        rows = [feature(4 * j + ff) if 4 * j + ff < 18 else jnp.zeros((32, LANES), jnp.float32) for ff in range(4)]
+        for oo, block in enumerate(exchange_quarters(rows, quarter)):
             if j == 3:
                 count = counts_col[pl.ds(oo, 32, stride=4), :]
                 live = (slot < count).astype(jnp.float32)
@@ -79,12 +91,8 @@
         for j in range(BACK_ROWS):
             from_row = 4 * BACK_ROWS * tiles * part + j
             blocks = [back_ref[pl.ds(from_row + BACK_ROWS * oo, tiles, stride=4 * BACK_ROWS), :] for oo in range(4)]
-            for ff in range(4):
+            for ff, row in enumerate(exchange_quarters(blocks, quarter)):
                 f = 4 * j + ff
-                row = blocks[0]
-                for oo, block in enumerate(blocks):
-                    moved = pltpu.roll(block, ((oo - ff) * CAP) % LANES, 1) if ff != oo else block
-                    row = jnp.where(quarter == oo, moved, row)
                 out_ref[f // 8, at, f % 8, :] = row
         piece = pl.ds(tiles * part, tiles)
         copies.append(pltpu.make_async_copy(out_ref.at[:, piece], out_hbm.at[:, piece], sems.at[part]))

time: 46 us -> 45.9 us (level)
  no operation moved by 1% of the time
where the time goes in v4:
time: 45.9 us; the launch traced here: 45.7 us
  blocking collectives  38.7 us (84%)
  Pallas kernels  6.3 us (14%)
  between operations  0.66 us (1%)
    all_to_all x1, blocking collectives, local(): lax.all_to_all(send.reshape(DEVS, 1, SEND_ROWS * LANES), ('drift', 'cross...  23.4 us
    all_to_all x1, blocking collectives, local(): lax.all_to_all(back.reshape(DEVS, 1, BACK_ROWS * LANES), ('drift', 'cross...  15.3 us
    pallas_call x1, Pallas kernels, local(): pl.pallas_call(steps_kernel, out_shape=(jax.ShapeDtypeStruct((DEVS * BACK...  4.15 us
    pallas_call x1, Pallas kernels, local(): pl.pallas_call(pack_kernel, out_shape=jax.ShapeDtypeStruct((DEVS * SEND_R...  1.24 us

profile of v4, /device:TPU:1, one launch (start us, length us, event | category | flops | bytes accessed | tf_op | source)
XLA Modules:
  0.0 45.7 jit_solution(3836415765698680159)
XLA Ops:
  0.6 1.2 %shard_map.68 = f32[640,128]{1,0:T(8,128)S(1)} custom-call(f32[2,32,8,128]{3,2,1,0:T(8,128)} %bitcast.19, s32[1,128]{1,0:T(1,128)} %bitcast.23, s32[32,128]{1,0:T(8,128)} %bitcast.21, s32[32,128]{1,0:T(8,128)} %bitcast.22), custom_call_target="tpu_custom_call" | custom-call | tf_op jit(solution)/shard_map/pallas_call | solution.py:339
  1.9 0.0 copy-start
  1.9 23.4 %all_to_all.10 = f32[128,1,640]{2,1,0:T(1,128)S(1)} all-to-all(f32[128,1,640]{2,1,0:T(1,128)S(1)} %bitcast.15), channel_id=1, replica_groups=mesh['drift'=8,'cross'=16] {'drift','cross'}, dimensions={0} | all-to-all | bytes 655360 | tf_op jit(solution)/shard_map/all_to_all | solution.py:354
  25.3 0.0 copy-done
  25.3 4.1 %shard_map.69 = (f32[512,128]{1,0:T(8,128)S(1)}, f32[3,4096]{1,0:T(4,128)}) custom-call(f32[640,128]{1,0:T(8,128)S(1)} %bitcast.14, f32[32,128]{1,0:T(8,128)S(1)} %bitcast.18), custom_call_target="tpu_custom_call" | custom-call | tf_op jit(solution)/shard_map/pallas_call | solution.py:357
  29.5 15.3 %all_to_all.11 = f32[128,1,512]{2,1,0:T(1,128)S(1)} all-to-all(f32[128,1,512]{2,1,0:T(1,128)S(1)} %bitcast.17), channel_id=1, replica_groups=mesh['drift'=8,'cross'=16] {'drift','cross'}, dimensions={0} | all-to-all | bytes 524288 | tf_op jit(solution)/shard_map/all_to_all | solution.py:381
  44.7 0.9 %shard_map.70 = f32[2,32,8,128]{3,2,1,0:T(8,128)} custom-call(f32[512,128]{1,0:T(8,128)S(1)} %bitcast.16), custom_call_target="tpu_custom_call" | custom-call | tf_op jit(solution)/shard_map/pallas_call | solution.py:384
Async XLA Ops:
  1.9 23.4 %copy-start = (f32[4096]{0:T(1024)S(1)}, f32[4096]{0:T(1024)}, u32[]{:S(2)}) copy-start(f32[4096]{0:T(1024)} %param.9) | copy-start | bytes 49156

commit v5 on v4

--- a/solution.py
+++ b/solution.py
@@ -53,17 +53,17 @@
 def pack_kernel(
     points_hbm, counts_hbm, first_hbm, second_hbm, out_ref, points_ref, counts_ref, first_ref, second_ref, counts_col, sems
 ):
-    moves = ((counts_hbm, counts_ref), (points_hbm, points_ref), (first_hbm, first_ref), (second_hbm, second_ref))
+    moves = ((points_hbm, points_ref), (first_hbm, first_ref), (second_hbm, second_ref), (counts_hbm, counts_ref))
     copies = [pltpu.make_async_copy(source, target, sems.at[n]) for n, (source, target) in enumerate(moves)]
     for copy in copies:
         copy.start()
     lane = lax.broadcasted_iota(jnp.int32, (32, LANES), 1)
     quarter = lane // CAP
     slot = (lane - 3 * CAP).astype(jnp.float32)
-    copies[0].wait()
+    copies[3].wait()
     counts = counts_ref[...].astype(jnp.float32)
     counts_col[...] = jnp.broadcast_to(counts, (DEVS, LANES)).T
-    for copy in copies[1:]:
+    for copy in copies[:3]:
         copy.wait()
 
     def feature(f):
@@ -116,6 +116,7 @@
     reduced,
     keep,
     pairs,
+    quads,
     vel,
     sem,
 ):
@@ -129,9 +130,9 @@
         state[j * LANES : (j + 1) * LANES, :] = got_ref[pl.ds(j, DEVS, stride=SEND_ROWS), :].T
 
     contact = contact_ref[...]
-    pairs[pl.ds(0, 32, stride=2), :] = contact
-    pairs[pl.ds(1, 32, stride=2), :] = pltpu.roll(contact, NODES, 1)
-    turned = jnp.concatenate([pairs[...], pairs[...]], axis=0).T
+    pairs[0, pl.ds(0, 32, stride=2), :] = contact
+    pairs[0, pl.ds(1, 32, stride=2), :] = pltpu.roll(contact, NODES, 1)
+    turned = jnp.concatenate([pairs[0], pairs[0]], axis=0).T
     keep[...] = 1.0 - turned[0:NODES, :]
 
     def half(rows):
@@ -233,8 +234,6 @@
             if v == 2:
                 value = value - STEP_DURATION * GRAVITY_ACCEL
             node.append(value * keep[...])
-        if when_node is not None:
-            when_node(node)
         for v in range(3):
             for o in range(3):
                 value = jnp.where(low_half, node[v][16 * o : 16 * o + 16], node[v][16 * o + 16 : 16 * o + 32])
@@ -243,6 +242,9 @@
                 at = 48 * v + 16 * o
                 parts[at : at + 16, 0:LANES] = high
                 parts[at : at + 16, LANES : 2 * LANES] = low
+
+        if when_node is not None:
+            when_node(node)
 
         def gather(group, unused):
             slots = [8 * group + u for u in range(8)]
@@ -310,10 +312,13 @@
     def send_velocity(node):
         lane = lax.broadcasted_iota(jnp.int32, (32, LANES), 1)
         for v in range(3):
-            pairs[...] = jnp.concatenate([node[v], node[v]], axis=0).T[0:BLK_DEV, :]
-            packed = jnp.where(lane < NODES, pairs[pl.ds(0, 32, stride=2), :], pairs[pl.ds(1, 32, stride=2), :])
-            for q in range(32):
-                vel[v : v + 1, q * LANES : (q + 1) * LANES] = packed[q : q + 1, :]
+            pairs[v] = jnp.concatenate([node[v], node[v]], axis=0).T[0:BLK_DEV, :]
+        for v in range(3):
+            even, odd = (pairs[v, pl.ds(p, 32, stride=2), :] for p in range(2))
+            packed = jnp.where(lane < NODES, even, odd)
+            quads[pl.ds(v, 32, stride=4), :] = packed
+        for q in range(32):
+            vel[:, q * LANES : (q + 1) * LANES] = quads[4 * q : 4 * q + 3, :]
         copy.start()
 
     one_step(17, send_velocity)
@@ -372,7 +377,8 @@
             pltpu.VMEM((144, 2 * LANES), jnp.bfloat16),
             pltpu.VMEM((9, ROW * CAP, LANES), jnp.float32),
             pltpu.VMEM((NODES, LANES), jnp.float32),
-            pltpu.VMEM((BLK_DEV, LANES), jnp.float32),
+            pltpu.VMEM((3, BLK_DEV, LANES), jnp.float32),
+            pltpu.VMEM((LANES, LANES), jnp.float32),
             pltpu.VMEM((3, BLK_DEV * NODES), jnp.float32),
             pltpu.SemaphoreType.DMA(()),
         ],

time: 45.9 us -> 45.8 us (level)
  no operation moved by 1% of the time
where the time goes in v5:
time: 45.8 us; the launch traced here: 45.6 us
  blocking collectives  38.7 us (84%)
  Pallas kernels  6.28 us (14%)
  between operations  0.66 us (1%)
    all_to_all x1, blocking collectives, local(): lax.all_to_all(send.reshape(DEVS, 1, SEND_ROWS * LANES), ('drift', 'cross...  23.4 us
    all_to_all x1, blocking collectives, local(): lax.all_to_all(back.reshape(DEVS, 1, BACK_ROWS * LANES), ('drift', 'cross...  15.3 us
    pallas_call x1, Pallas kernels, local(): pl.pallas_call(steps_kernel, out_shape=(jax.ShapeDtypeStruct((DEVS * BACK...  4.15 us
    pallas_call x1, Pallas kernels, local(): pl.pallas_call(pack_kernel, out_shape=jax.ShapeDtypeStruct((DEVS * SEND_R...  1.23 us

profile of v5, /device:TPU:1, one launch (start us, length us, event | category | flops | bytes accessed | tf_op | source)
XLA Modules:
  0.0 45.6 jit_solution(13506716635359672805)
XLA Ops:
  0.6 1.2 %shard_map.68 = f32[640,128]{1,0:T(8,128)S(1)} custom-call(f32[2,32,8,128]{3,2,1,0:T(8,128)} %bitcast.19, s32[1,128]{1,0:T(1,128)} %bitcast.23, s32[32,128]{1,0:T(8,128)} %bitcast.21, s32[32,128]{1,0:T(8,128)} %bitcast.22), custom_call_target="tpu_custom_call" | custom-call | tf_op jit(solution)/shard_map/pallas_call | solution.py:344
  1.9 0.0 copy-start
  1.9 23.4 %all_to_all.10 = f32[128,1,640]{2,1,0:T(1,128)S(1)} all-to-all(f32[128,1,640]{2,1,0:T(1,128)S(1)} %bitcast.15), channel_id=1, replica_groups=mesh['drift'=8,'cross'=16] {'drift','cross'}, dimensions={0} | all-to-all | bytes 655360 | tf_op jit(solution)/shard_map/all_to_all | solution.py:359
  25.3 0.0 copy-done
  25.3 4.1 %shard_map.69 = (f32[512,128]{1,0:T(8,128)S(1)}, f32[3,4096]{1,0:T(4,128)}) custom-call(f32[640,128]{1,0:T(8,128)S(1)} %bitcast.14, f32[32,128]{1,0:T(8,128)S(1)} %bitcast.18), custom_call_target="tpu_custom_call" | custom-call | tf_op jit(solution)/shard_map/pallas_call | solution.py:362
  29.5 15.3 %all_to_all.11 = f32[128,1,512]{2,1,0:T(1,128)S(1)} all-to-all(f32[128,1,512]{2,1,0:T(1,128)S(1)} %bitcast.17), channel_id=1, replica_groups=mesh['drift'=8,'cross'=16] {'drift','cross'}, dimensions={0} | all-to-all | bytes 524288 | tf_op jit(solution)/shard_map/all_to_all | solution.py:387
  44.7 0.9 %shard_map.70 = f32[2,32,8,128]{3,2,1,0:T(8,128)} custom-call(f32[512,128]{1,0:T(8,128)S(1)} %bitcast.16), custom_call_target="tpu_custom_call" | custom-call | tf_op jit(solution)/shard_map/pallas_call | solution.py:390
Async XLA Ops:
  1.9 23.4 %copy-start = (f32[4096]{0:T(1024)S(1)}, f32[4096]{0:T(1024)}, u32[]{:S(2)}) copy-start(f32[4096]{0:T(1024)} %param.9) | copy-start | bytes 49156

commit v6 on v5

--- a/solution.py
+++ b/solution.py
@@ -149,9 +149,7 @@
     j_of = (sub // 4).astype(jnp.float32)
 
     def one_step(ids_row, when_node=None):
-        sums[...] = jnp.zeros_like(sums)
-
-        def scatter(group, unused):
+        def scatter(group):
             def feature(f):
                 return state[pl.ds(pl.multiple_of(f * CAP + 8 * group, 8), 8), :]
 
@@ -204,15 +202,16 @@
                 one = chosen(cells[pl.ds(8 * group + u, 1), :], 2 * BLK_DEV)
                 terms += [high, low]
                 selectors += [one, one]
-            sums[...] += lax.dot_general(
+            return lax.dot_general(
                 jnp.concatenate(terms, axis=1),
                 jnp.concatenate(selectors, axis=1),
                 (((1,), (1,)), ((), ())),
                 preferred_element_type=jnp.float32,
             )
-            return unused
-
-        lax.fori_loop(0, CAP // 8, scatter, 0, unroll=4)
+
+        for group in range(CAP // 8):
+            part = scatter(group)
+            sums[...] = part if group == 0 else sums[...] + part
 
         low_half = half(16)
         for f in range(4):

time: 45.8 us -> 45.8 us (level)
  no operation moved by 1% of the time
where the time goes in v6:
time: 45.8 us; the launch traced here: 45.6 us
  blocking collectives  38.7 us (84%)
  Pallas kernels  6.26 us (14%)
  between operations  0.66 us (1%)
    all_to_all x1, blocking collectives, local(): lax.all_to_all(send.reshape(DEVS, 1, SEND_ROWS * LANES), ('drift', 'cross...  23.4 us
    all_to_all x1, blocking collectives, local(): lax.all_to_all(back.reshape(DEVS, 1, BACK_ROWS * LANES), ('drift', 'cross...  15.3 us
    pallas_call x1, Pallas kernels, local(): pl.pallas_call(steps_kernel, out_shape=(jax.ShapeDtypeStruct((DEVS * BACK...  4.13 us
    pallas_call x1, Pallas kernels, local(): pl.pallas_call(pack_kernel, out_shape=jax.ShapeDtypeStruct((DEVS * SEND_R...  1.23 us

profile of v6, /device:TPU:1, one launch (start us, length us, event | category | flops | bytes accessed | tf_op | source)
XLA Modules:
  0.0 45.6 jit_solution(13184801224164294397)
XLA Ops:
  0.6 1.2 %shard_map.68 = f32[640,128]{1,0:T(8,128)S(1)} custom-call(f32[2,32,8,128]{3,2,1,0:T(8,128)} %bitcast.19, s32[1,128]{1,0:T(1,128)} %bitcast.23, s32[32,128]{1,0:T(8,128)} %bitcast.21, s32[32,128]{1,0:T(8,128)} %bitcast.22), custom_call_target="tpu_custom_call" | custom-call | tf_op jit(solution)/shard_map/pallas_call | solution.py:343
  1.9 0.0 copy-start
  1.9 23.4 %all_to_all.10 = f32[128,1,640]{2,1,0:T(1,128)S(1)} all-to-all(f32[128,1,640]{2,1,0:T(1,128)S(1)} %bitcast.15), channel_id=1, replica_groups=mesh['drift'=8,'cross'=16] {'drift','cross'}, dimensions={0} | all-to-all | bytes 655360 | tf_op jit(solution)/shard_map/all_to_all | solution.py:358
  25.3 0.0 copy-done
  25.3 4.1 %shard_map.69 = (f32[512,128]{1,0:T(8,128)S(1)}, f32[3,4096]{1,0:T(4,128)}) custom-call(f32[640,128]{1,0:T(8,128)S(1)} %bitcast.14, f32[32,128]{1,0:T(8,128)S(1)} %bitcast.18), custom_call_target="tpu_custom_call" | custom-call | tf_op jit(solution)/shard_map/pallas_call | solution.py:361
  29.5 15.3 %all_to_all.11 = f32[128,1,512]{2,1,0:T(1,128)S(1)} all-to-all(f32[128,1,512]{2,1,0:T(1,128)S(1)} %bitcast.17), channel_id=1, replica_groups=mesh['drift'=8,'cross'=16] {'drift','cross'}, dimensions={0} | all-to-all | bytes 524288 | tf_op jit(solution)/shard_map/all_to_all | solution.py:386
  44.7 0.9 %shard_map.70 = f32[2,32,8,128]{3,2,1,0:T(8,128)} custom-call(f32[512,128]{1,0:T(8,128)S(1)} %bitcast.16), custom_call_target="tpu_custom_call" | custom-call | tf_op jit(solution)/shard_map/pallas_call | solution.py:389
Async XLA Ops:
  1.9 23.4 %copy-start = (f32[4096]{0:T(1024)S(1)}, f32[4096]{0:T(1024)}, u32[]{:S(2)}) copy-start(f32[4096]{0:T(1024)} %param.9) | copy-start | bytes 49156

commit v7 on v5

--- a/solution.py
+++ b/solution.py
@@ -143,6 +143,10 @@
 
     def chosen(row, rows):
         return jnp.where(numbers(rows) == row, 1.0, 0.0).astype(jnp.bfloat16)
+
+    def chosen_narrow(row, rows):
+        one, none = jnp.bfloat16(1.0), jnp.bfloat16(0.0)
+        return jnp.where(numbers(rows).astype(jnp.bfloat16) == row.astype(jnp.bfloat16), one, none)
 
     sub = lax.broadcasted_iota(jnp.int32, (8, LANES), 0)
     k_of = (sub % 4).astype(jnp.float32)
@@ -248,7 +252,7 @@
 
         def gather(group, unused):
             slots = [8 * group + u for u in range(8)]
-            selectors = [chosen(cells[pl.ds(c, 1), :], 2 * BLK_DEV) for c in slots]
+            selectors = [chosen_narrow(cells[pl.ds(c, 1), :], 2 * BLK_DEV) for c in slots]
             selector = jnp.concatenate(selectors, axis=1)
             nodal_all = jnp.dot(
                 parts[...], jnp.concatenate([selector, selector], axis=0), preferred_element_type=jnp.float32

time: 45.8 us -> 45.8 us (level)
  no operation moved by 1% of the time
where the time goes in v7:
time: 45.8 us; the launch traced here: 45.6 us
  blocking collectives  38.7 us (84%)
  Pallas kernels  6.27 us (14%)
  between operations  0.66 us (1%)
    all_to_all x1, blocking collectives, local(): lax.all_to_all(send.reshape(DEVS, 1, SEND_ROWS * LANES), ('drift', 'cross...  23.4 us
    all_to_all x1, blocking collectives, local(): lax.all_to_all(back.reshape(DEVS, 1, BACK_ROWS * LANES), ('drift', 'cross...  15.3 us
    pallas_call x1, Pallas kernels, local(): pl.pallas_call(steps_kernel, out_shape=(jax.ShapeDtypeStruct((DEVS * BACK...  4.13 us
    pallas_call x1, Pallas kernels, local(): pl.pallas_call(pack_kernel, out_shape=jax.ShapeDtypeStruct((DEVS * SEND_R...  1.23 us

profile of v7, /device:TPU:1, one launch (start us, length us, event | category | flops | bytes accessed | tf_op | source)
XLA Modules:
  0.0 45.6 jit_solution(9155088118641901439)
XLA Ops:
  0.6 1.2 %shard_map.68 = f32[640,128]{1,0:T(8,128)S(1)} custom-call(f32[2,32,8,128]{3,2,1,0:T(8,128)} %bitcast.19, s32[1,128]{1,0:T(1,128)} %bitcast.23, s32[32,128]{1,0:T(8,128)} %bitcast.21, s32[32,128]{1,0:T(8,128)} %bitcast.22), custom_call_target="tpu_custom_call" | custom-call | tf_op jit(solution)/shard_map/pallas_call | solution.py:348
  1.9 0.0 copy-start
  1.9 23.4 %all_to_all.10 = f32[128,1,640]{2,1,0:T(1,128)S(1)} all-to-all(f32[128,1,640]{2,1,0:T(1,128)S(1)} %bitcast.15), channel_id=1, replica_groups=mesh['drift'=8,'cross'=16] {'drift','cross'}, dimensions={0} | all-to-all | bytes 655360 | tf_op jit(solution)/shard_map/all_to_all | solution.py:363
  25.3 0.0 copy-done
  25.3 4.1 %shard_map.69 = (f32[512,128]{1,0:T(8,128)S(1)}, f32[3,4096]{1,0:T(4,128)}) custom-call(f32[640,128]{1,0:T(8,128)S(1)} %bitcast.14, f32[32,128]{1,0:T(8,128)S(1)} %bitcast.18), custom_call_target="tpu_custom_call" | custom-call | tf_op jit(solution)/shard_map/pallas_call | solution.py:366
  29.5 15.3 %all_to_all.11 = f32[128,1,512]{2,1,0:T(1,128)S(1)} all-to-all(f32[128,1,512]{2,1,0:T(1,128)S(1)} %bitcast.17), channel_id=1, replica_groups=mesh['drift'=8,'cross'=16] {'drift','cross'}, dimensions={0} | all-to-all | bytes 524288 | tf_op jit(solution)/shard_map/all_to_all | solution.py:391
  44.7 0.9 %shard_map.70 = f32[2,32,8,128]{3,2,1,0:T(8,128)} custom-call(f32[512,128]{1,0:T(8,128)S(1)} %bitcast.16), custom_call_target="tpu_custom_call" | custom-call | tf_op jit(solution)/shard_map/pallas_call | solution.py:394
Async XLA Ops:
  1.9 23.4 %copy-start = (f32[4096]{0:T(1024)S(1)}, f32[4096]{0:T(1024)}, u32[]{:S(2)}) copy-start(f32[4096]{0:T(1024)} %param.9) | copy-start | bytes 49156
